TPU v7x, 32 devices: a whole 2x2x4 slice. The times are simulated.
32 devices in a mesh: blk: 16 (over z, y, core), grp: 2 (over x).
Axes of the slice: x: 2, y: 2, z: 4, core: 2. Of those that a mesh axis runs over, the one named last changes fastest.
Arguments:
- features: bfloat16 [2, 16384, 2048], P('grp', 'blk'), may hold values from -6 to 6
- neighbours: int32 [2, 16384, 64], P('grp', 'blk'), may hold values from 0 to 1535
- degree: int32 [2, 16384], P('grp', 'blk'), may hold values from 16 to 64, as said below
- weight_one: bfloat16 [2048, 2048], replicated, may hold values from -0.5 to 0.5
- bias_one: float32 [2048], replicated, may hold values from -3 to 3
- weight_two: bfloat16 [2048, 2048], replicated, may hold values from -0.5 to 0.5
- bias_two: float32 [2048], replicated, may hold values from -3 to 3
- cotangent: bfloat16 [2, 16384, 2048], P('grp', 'blk'), may hold values from -6 to 6
Outputs:
- activations: bfloat16 [2, 16384, 2048], P('grp', 'blk')
- input_grad: bfloat16 [2, 16384, 2048], P('grp', 'blk')
- grad_weight_one: float32 [2048, 2048], P(('blk', 'grp'))
- grad_bias_one: float32 [2048], P(('blk', 'grp'))
- grad_weight_two: float32 [2048, 2048], P(('blk', 'grp'))
- grad_bias_two: float32 [2048], P(('blk', 'grp'))
Inputs may be any that keep to these rules, and one draw needn't show every extreme that they name: `degree`: used slots of a node's neighbour list; in each block of 1024 nodes some node uses all 64. `neighbours`: rows of the node's window: the last 256 nodes of the previous block, the 1024 nodes of its own, then the first 256 of the next; unused slots hold arbitrary rows.
All inputs are finite; a program needn't handle non-finite values.
Results may differ from a plain program's by a relative error of at most 0.013.
Values may be sent and summed in bfloat16 or wider, within the bound.
No kernel may reach another device: no remote copies, remote signals or barrier semaphores. Data moves between devices by JAX's collectives and lax.ppermute only.
A program may use at most 192 MiB of HBM per device.

v0:
```python
import jax
import jax.numpy as jnp
from jax import lax
from jax.sharding import PartitionSpec as P

BAND = 256


def extended(cells, sides, width):
    for axis, dim in sides:
        count = lax.axis_size(axis)
        head = lax.slice_in_dim(cells, 0, width, axis=dim)
        tail = lax.slice_in_dim(cells, cells.shape[dim] - width, cells.shape[dim], axis=dim)
        cells = jnp.concatenate(
            [
                lax.ppermute(tail, axis, [(i, (i + 1) % count) for i in range(count)]),
                cells,
                lax.ppermute(head, axis, [((i + 1) % count, i) for i in range(count)]),
            ],
            axis=dim,
        )
    return cells


def passed_along(block, axis, distance):
    devices = range(lax.axis_size(axis))
    route = [((i - distance) % len(devices), i) for i in devices]
    return lax.ppermute(block, axis, route)


def count_table(slots, degree):
    row_count = slots.shape[0]
    slot_total = slots.shape[1]
    width = row_count + 2 * BAND
    slot_ids = lax.broadcasted_iota(jnp.int32, slots.shape, 1)
    slot_used = (slot_ids < degree[:, None]).astype(jnp.float32)
    columns = lax.broadcasted_iota(jnp.int32, (1, 1, width), 2)

    def add_block(step, counts):
        start = step * 4
        block_slots = lax.dynamic_slice_in_dim(slots, start, 4, 1)
        block_used = lax.dynamic_slice_in_dim(slot_used, start, 4, 1)
        match = (block_slots[:, :, None] == columns).astype(jnp.float32)
        return counts + jnp.sum(match * block_used[:, :, None], axis=1)

    counts = lax.fori_loop(
        0, slot_total // 4, add_block, jnp.zeros((row_count, width), jnp.float32)
    )
    return counts.astype(jnp.bfloat16)


def cycle_window(field):
    return extended(field, (("blk", 0),), BAND)


def aggregate(window, field, counts, degree_plus, weight, bias_vec):
    neighbour_sum = jnp.dot(counts, window, preferred_element_type=jnp.float32)
    pre_sum = neighbour_sum + 2.0 * field.astype(jnp.float32)
    averaged = (pre_sum / degree_plus).astype(jnp.bfloat16)
    preact = jnp.dot(averaged, weight, preferred_element_type=jnp.float32) + bias_vec
    return (averaged, preact)


def reduce_grads(grad_weight, grad_bias):
    return (
        lax.psum_scatter(grad_weight, ("blk", "grp"), scatter_dimension=0, tiled=True),
        lax.psum_scatter(grad_bias, ("blk", "grp"), scatter_dimension=0, tiled=True),
    )


def layer_back(grad_out, preact, averaged, counts, degree_plus, weight):
    node_count = averaged.shape[0]
    _, gelu_pull = jax.vjp(jax.nn.gelu, preact)
    grad_pre = gelu_pull(grad_out)[0].astype(jnp.bfloat16)
    grad_weight = lax.dot_general(
        averaged, grad_pre, (((0,), (0,)), ((), ())), preferred_element_type=jnp.float32
    )
    grad_bias = jnp.sum(grad_pre.astype(jnp.float32), axis=0)
    summed = reduce_grads(grad_weight, grad_bias)
    grad_avg = lax.dot_general(
        grad_pre, weight, (((1,), (1,)), ((), ())), preferred_element_type=jnp.float32
    )
    grad_scaled = (grad_avg / degree_plus).astype(jnp.bfloat16)
    grad_window = lax.dot_general(
        counts, grad_scaled, (((0,), (0,)), ((), ())), preferred_element_type=jnp.float32
    )
    from_next = passed_along(grad_window[:BAND].astype(jnp.bfloat16), "blk", -1).astype(jnp.float32)
    from_prev = passed_along(
        grad_window[BAND + node_count :].astype(jnp.bfloat16), "blk", 1
    ).astype(jnp.float32)
    grad_in = grad_window[BAND : BAND + node_count] + 2.0 * grad_scaled.astype(jnp.float32)
    grad_in = grad_in.at[:BAND].add(from_prev).at[node_count - BAND :].add(from_next)
    return (grad_in, summed[0], summed[1])


def local(features, neighbours, degree, weight_one, bias_one, weight_two, bias_two, cotangent):
    field_zero = features[0]
    own_degree = degree[0]
    counts = count_table(neighbours[0], own_degree)
    degree_plus = own_degree.astype(jnp.float32)[:, None] + 1.0
    averaged_one, preact_one = aggregate(
        cycle_window(field_zero), field_zero, counts, degree_plus, weight_one, bias_one
    )
    hidden = jax.nn.gelu(preact_one).astype(jnp.bfloat16)
    averaged_two, preact_two = aggregate(
        cycle_window(hidden), hidden, counts, degree_plus, weight_two, bias_two
    )
    activations = jax.nn.gelu(preact_two).astype(jnp.bfloat16)
    grad_hidden, grad_w_two, grad_b_two = layer_back(
        cotangent[0].astype(jnp.float32), preact_two, averaged_two, counts, degree_plus, weight_two
    )
    grad_input, grad_w_one, grad_b_one = layer_back(
        grad_hidden, preact_one, averaged_one, counts, degree_plus, weight_one
    )
    return (
        activations[None],
        grad_input.astype(jnp.bfloat16)[None],
        grad_w_one,
        grad_b_one,
        grad_w_two,
        grad_b_two,
    )


def solution(mesh):
    return jax.shard_map(
        local,
        mesh=mesh,
        in_specs=(
            P("grp", "blk", None),
            P("grp", "blk", None),
            P("grp", "blk"),
            P(),
            P(),
            P(),
            P(),
            P("grp", "blk", None),
        ),
        out_specs=(
            P("grp", "blk", None),
            P("grp", "blk", None),
            P(("blk", "grp"), None),
            P(("blk", "grp")),
            P(("blk", "grp"), None),
            P(("blk", "grp")),
        ),
        check_vma=False,
    )
```

profile of v0, /device:TPU:18, one launch (start us, length us, event | category | flops | bytes accessed | tf_op | source)
XLA Modules:
  0.0 1158.4 jit_solution(17322084236498759436)
XLA Ops:
  9.0 2.6 collective-permute-start.1
  12.3 326.2 %while.18 = (s32[]{:T(128)}, f32[1024,1536]{1,0:T(8,128)}, s32[1024,64]{0,1:T(8,128)}, f32[1024,64]{0,1:T(8,128)S(1)}, s32[]{:T(128)}, /*index=5*/s32[]{:T(128)}, s32[]{:T(128)}, s32[]{:T(128)}) while((s32[]{:T(128)}, f32[1024,1536]{1,0:T(8,128)}, s32[1024,64]{0,1:T(8,128)}, f32[1024,64]{0,1:T(8,128)S(1)}, s32[]{:T(128)}, ...), condition=%wide.region_2.0_spmd.clone, body=%wide.region_0.0_spmd.clone.sunk | while | flops 20447236 | bytes 75595984 | solution.py:46
  13.3 14.6 %select_reduce_fusion.2 = f32[1024,1536]{1,0:T(8,128)S(1)} fusion(f32[1024,4]{0,1:T(4,128)S(1)} %constant_dynamic-slice_fusion.4, s32[1024,4]{0,1:T(4,128)S(1)} %constant_dynamic-slice_fusion.5), kind=kLoop, calls=%fused_computation.2.clone.1 | loop fusion | flops 17301504 | bytes 6324224 | tf_op jit(solution)/shard_map/while/body/eval_jaxpr/reduce_sum | solution.py:44
  27.9 2.1 select_add_fusion.2
  30.1 2.6 copy-done.1
  33.7 14.6 %select_reduce_fusion.2 = f32[1024,1536]{1,0:T(8,128)S(1)} fusion(f32[1024,4]{0,1:T(4,128)S(1)} %constant_dynamic-slice_fusion.4, s32[1024,4]{0,1:T(4,128)S(1)} %constant_dynamic-slice_fusion.5), kind=kLoop, calls=%fused_computation.2.clone.1 | loop fusion | flops 17301504 | bytes 6324224 | tf_op jit(solution)/shard_map/while/body/eval_jaxpr/reduce_sum | solution.py:44
  48.3 2.1 select_add_fusion.2
  50.5 2.6 copy-done.1
  54.0 14.6 %select_reduce_fusion.2 = f32[1024,1536]{1,0:T(8,128)S(1)} fusion(f32[1024,4]{0,1:T(4,128)S(1)} %constant_dynamic-slice_fusion.4, s32[1024,4]{0,1:T(4,128)S(1)} %constant_dynamic-slice_fusion.5), kind=kLoop, calls=%fused_computation.2.clone.1 | loop fusion | flops 17301504 | bytes 6324224 | tf_op jit(solution)/shard_map/while/body/eval_jaxpr/reduce_sum | solution.py:44
  68.7 2.1 select_add_fusion.2
  70.9 2.6 copy-done.1
  74.4 14.6 %select_reduce_fusion.2 = f32[1024,1536]{1,0:T(8,128)S(1)} fusion(f32[1024,4]{0,1:T(4,128)S(1)} %constant_dynamic-slice_fusion.4, s32[1024,4]{0,1:T(4,128)S(1)} %constant_dynamic-slice_fusion.5), kind=kLoop, calls=%fused_computation.2.clone.1 | loop fusion | flops 17301504 | bytes 6324224 | tf_op jit(solution)/shard_map/while/body/eval_jaxpr/reduce_sum | solution.py:44
  89.1 2.1 select_add_fusion.2
  91.3 2.6 copy-done.1
  94.8 14.6 %select_reduce_fusion.2 = f32[1024,1536]{1,0:T(8,128)S(1)} fusion(f32[1024,4]{0,1:T(4,128)S(1)} %constant_dynamic-slice_fusion.4, s32[1024,4]{0,1:T(4,128)S(1)} %constant_dynamic-slice_fusion.5), kind=kLoop, calls=%fused_computation.2.clone.1 | loop fusion | flops 17301504 | bytes 6324224 | tf_op jit(solution)/shard_map/while/body/eval_jaxpr/reduce_sum | solution.py:44
  111.6 2.6 copy-done.1
  115.2 14.6 %select_reduce_fusion.2 = f32[1024,1536]{1,0:T(8,128)S(1)} fusion(f32[1024,4]{0,1:T(4,128)S(1)} %constant_dynamic-slice_fusion.4, s32[1024,4]{0,1:T(4,128)S(1)} %constant_dynamic-slice_fusion.5), kind=kLoop, calls=%fused_computation.2.clone.1 | loop fusion | flops 17301504 | bytes 6324224 | tf_op jit(solution)/shard_map/while/body/eval_jaxpr/reduce_sum | solution.py:44
  132.0 2.6 copy-done.1
  135.6 14.6 %select_reduce_fusion.2 = f32[1024,1536]{1,0:T(8,128)S(1)} fusion(f32[1024,4]{0,1:T(4,128)S(1)} %constant_dynamic-slice_fusion.4, s32[1024,4]{0,1:T(4,128)S(1)} %constant_dynamic-slice_fusion.5), kind=kLoop, calls=%fused_computation.2.clone.1 | loop fusion | flops 17301504 | bytes 6324224 | tf_op jit(solution)/shard_map/while/body/eval_jaxpr/reduce_sum | solution.py:44
  152.4 2.6 copy-done.1
  156.0 14.6 %select_reduce_fusion.2 = f32[1024,1536]{1,0:T(8,128)S(1)} fusion(f32[1024,4]{0,1:T(4,128)S(1)} %constant_dynamic-slice_fusion.4, s32[1024,4]{0,1:T(4,128)S(1)} %constant_dynamic-slice_fusion.5), kind=kLoop, calls=%fused_computation.2.clone.1 | loop fusion | flops 17301504 | bytes 6324224 | tf_op jit(solution)/shard_map/while/body/eval_jaxpr/reduce_sum | solution.py:44
  172.8 2.6 copy-done.1
  176.3 14.6 %select_reduce_fusion.2 = f32[1024,1536]{1,0:T(8,128)S(1)} fusion(f32[1024,4]{0,1:T(4,128)S(1)} %constant_dynamic-slice_fusion.4, s32[1024,4]{0,1:T(4,128)S(1)} %constant_dynamic-slice_fusion.5), kind=kLoop, calls=%fused_computation.2.clone.1 | loop fusion | flops 17301504 | bytes 6324224 | tf_op jit(solution)/shard_map/while/body/eval_jaxpr/reduce_sum | solution.py:44
  193.2 2.6 copy-done.1
  196.7 14.6 %select_reduce_fusion.2 = f32[1024,1536]{1,0:T(8,128)S(1)} fusion(f32[1024,4]{0,1:T(4,128)S(1)} %constant_dynamic-slice_fusion.4, s32[1024,4]{0,1:T(4,128)S(1)} %constant_dynamic-slice_fusion.5), kind=kLoop, calls=%fused_computation.2.clone.1 | loop fusion | flops 17301504 | bytes 6324224 | tf_op jit(solution)/shard_map/while/body/eval_jaxpr/reduce_sum | solution.py:44
  213.6 2.6 copy-done.1
  217.1 14.6 %select_reduce_fusion.2 = f32[1024,1536]{1,0:T(8,128)S(1)} fusion(f32[1024,4]{0,1:T(4,128)S(1)} %constant_dynamic-slice_fusion.4, s32[1024,4]{0,1:T(4,128)S(1)} %constant_dynamic-slice_fusion.5), kind=kLoop, calls=%fused_computation.2.clone.1 | loop fusion | flops 17301504 | bytes 6324224 | tf_op jit(solution)/shard_map/while/body/eval_jaxpr/reduce_sum | solution.py:44
  233.9 2.6 copy-done.1
  237.5 14.6 %select_reduce_fusion.2 = f32[1024,1536]{1,0:T(8,128)S(1)} fusion(f32[1024,4]{0,1:T(4,128)S(1)} %constant_dynamic-slice_fusion.4, s32[1024,4]{0,1:T(4,128)S(1)} %constant_dynamic-slice_fusion.5), kind=kLoop, calls=%fused_computation.2.clone.1 | loop fusion | flops 17301504 | bytes 6324224 | tf_op jit(solution)/shard_map/while/body/eval_jaxpr/reduce_sum | solution.py:44
  254.3 2.6 copy-done.1
  257.9 14.6 %select_reduce_fusion.2 = f32[1024,1536]{1,0:T(8,128)S(1)} fusion(f32[1024,4]{0,1:T(4,128)S(1)} %constant_dynamic-slice_fusion.4, s32[1024,4]{0,1:T(4,128)S(1)} %constant_dynamic-slice_fusion.5), kind=kLoop, calls=%fused_computation.2.clone.1 | loop fusion | flops 17301504 | bytes 6324224 | tf_op jit(solution)/shard_map/while/body/eval_jaxpr/reduce_sum | solution.py:44
  274.7 2.6 copy-done.1
  278.3 14.6 %select_reduce_fusion.2 = f32[1024,1536]{1,0:T(8,128)S(1)} fusion(f32[1024,4]{0,1:T(4,128)S(1)} %constant_dynamic-slice_fusion.4, s32[1024,4]{0,1:T(4,128)S(1)} %constant_dynamic-slice_fusion.5), kind=kLoop, calls=%fused_computation.2.clone.1 | loop fusion | flops 17301504 | bytes 6324224 | tf_op jit(solution)/shard_map/while/body/eval_jaxpr/reduce_sum | solution.py:44
  295.1 2.6 copy-done.1
  298.6 14.6 %select_reduce_fusion.2 = f32[1024,1536]{1,0:T(8,128)S(1)} fusion(f32[1024,4]{0,1:T(4,128)S(1)} %constant_dynamic-slice_fusion.4, s32[1024,4]{0,1:T(4,128)S(1)} %constant_dynamic-slice_fusion.5), kind=kLoop, calls=%fused_computation.2.clone.1 | loop fusion | flops 17301504 | bytes 6324224 | tf_op jit(solution)/shard_map/while/body/eval_jaxpr/reduce_sum | solution.py:44
  315.5 2.6 copy-done.1
  319.0 14.6 %select_reduce_fusion.2 = f32[1024,1536]{1,0:T(8,128)S(1)} fusion(f32[1024,4]{0,1:T(4,128)S(1)} %constant_dynamic-slice_fusion.4, s32[1024,4]{0,1:T(4,128)S(1)} %constant_dynamic-slice_fusion.5), kind=kLoop, calls=%fused_computation.2.clone.1 | loop fusion | flops 17301504 | bytes 6324224 | tf_op jit(solution)/shard_map/while/body/eval_jaxpr/reduce_sum | solution.py:44
  335.9 2.6 copy-done.1
  338.5 3.3 convert_element_type.84
  342.5 9.6 divide_convert_fusion.3
  352.1 12.7 %multiply_convert_fusion.1 = (bf16[1024,2048]{1,0:T(8,128)(2,1)S(1)}, f32[1024,2048]{1,0:T(8,128)}) fusion(f32[2048]{0:T(1024)S(1)} %copy-done.9, bf16[1024,2048]{1,0:T(8,128)(2,1)S(1)} %divide_convert_fusion.3, bf16[2048,2048]{1,0:T(8,128)(2,1)S(1)} %bitcast.40), kind=kOutput, calls=%fused_computation.37 | convolution fusion | flops 8610906112 | bytes 25174016 | tf_op jit(solution)/shard_map/dot_general | solution.py:60
  365.4 2.6 collective-permute-start.3
  368.0 12.5 %collective-permute-done.2 = bf16[256,2048]{1,0:T(8,128)(2,1)S(1)} collective-permute-done((bf16[256,2048]{1,0:T(8,128)(2,1)S(1)}, bf16[256,2048]{1,0:T(8,128)(2,1)S(1)}, u32[]{:S(2)}, u32[]{:S(2)}) %collective-permute-start.2) | collective-permute-done | bytes 1048608 | tf_op jit(solution)/shard_map/ppermute | solution.py:16
  380.6 8.3 divide_convert_fusion.2
  388.9 18.5 %convert_reduce_fusion = (f32[2048]{0:T(1024)S(1)}, bf16[1024,2048]{1,0:T(8,128)(2,1)S(1)}, bf16[1,1024,2048]{2,1,0:T(8,128)(2,1)}) fusion(f32[2048]{0:T(1024)S(1)} %copy-done.11, bf16[1,1024,2048]{2,1,0:T(8,128)(2,1)S(1)} %copy-done.10, bf16[1024,2048]{1,0:T(8,128)(2,1)} %divide_convert_fusion.2, bf16[2048,2048]{1,0:T(8,128)(2,1)S(1)} %bitcast.38), kind=kOutput, calls=%fused_computation.31 | convolution fusion | flops 8644458496 | bytes 25182208 | tf_op jit(solution)/shard_map/dot_general | solution.py:60
  409.4 11.5 fusion.51
  421.4 12.7 %divide_convert_fusion.1 = bf16[1024,2048]{1,0:T(8,128)(2,1)S(1)} fusion(f32[1024]{0:T(1024)S(1)} %convert_add_fusion, bf16[1024,2048]{1,0:T(8,128)(2,1)} %copy-done.14, bf16[2048,2048]{1,0:T(8,128)(2,1)} %param.23), kind=kOutput, calls=%fused_computation.34 | convolution fusion | flops 8594128896 | bytes 16781312 | tf_op jit(solution)/shard_map/dot_general | solution.py:80
  434.1 9.2 fusion.48
  444.7 11.0 collective-permute-start.4
  455.7 4.7 slice_add_fusion.1
  460.4 3.8 collective-permute-done.4
  466.0 5.5 collective-permute-done.5
  472.0 8.5 convert_reduce_fusion.1
  482.5 11.7 %fusion.50 = f32[2048,2048]{1,0:T(8,128)} fusion(bf16[1024,2048]{1,0:T(8,128)(2,1)S(1)} %copy-done.13, bf16[1024,2048]{1,0:T(8,128)(2,1)S(1)} %get-tuple-element.179), kind=kOutput, calls=%fused_computation.73 | convolution fusion | flops 8589934592 | bytes 25165824 | tf_op jit(solution)/shard_map/dot_general | solution.py:75
  494.2 12.8 %divide_convert_fusion = bf16[1024,2048]{1,0:T(8,128)(2,1)S(1)} fusion(f32[1024]{0:T(1024)S(1)} %convert_add_fusion, bf16[1024,2048]{1,0:T(8,128)(2,1)} %copy-done.3, bf16[2048,2048]{1,0:T(8,128)(2,1)} %param.21), kind=kOutput, calls=%fused_computation.33 | convolution fusion | flops 8594128896 | bytes 16781312 | tf_op jit(solution)/shard_map/dot_general | solution.py:80
  507.0 9.1 fusion.49
  517.3 16.9 %collective-permute-start.6 = (bf16[256,2048]{1,0:T(8,128)(2,1)}, bf16[256,2048]{1,0:T(8,128)(2,1)S(1)}, u32[]{:S(2)}, u32[]{:S(2)}) collective-permute-start(bf16[256,2048]{1,0:T(8,128)(2,1)} %get-tuple-element.182), channel_id=1, source_target_pairs={{30,0},{0,2},{2,4},{4,6},{6,8},{8,10},{10,12},{12,14},{14,16},{16,... | collective-permute-start | bytes 3145736 | tf_op jit(solution)/shard_map/ppermute | solution.py:28
  534.2 10.1 slice_add_fusion
  544.3 54.3 %all-reduce.2 = (f32[2048]{0:T(1024)S(1)}, f32[2048]{0:T(1024)S(1)}) all-reduce(f32[2048]{0:T(1024)S(1)} %get-tuple-element.178, f32[2048]{0:T(1024)S(1)} %get-tuple-element.176), channel_id=3, replica_groups=mesh['blk'=16,'grp'=2] {'blk','grp'}, use_global_device_ids=true, to_apply=%region_5.0.clone | all-reduce | flops 4096 | bytes 32768
  599.8 3.3 fusion.33
  603.1 3.3 fusion.32
  606.4 6.1 convert_bitcast_fusion
  612.5 177.1 %reduce-scatter.5.cloned.1.call-done = f32[64,2048]{1,0:T(8,128)} async-done(((f32[2048,2048]{1,0:T(8,128)}), f32[64,2048]{1,0:T(8,128)}) %reduce-scatter.5.cloned.1.call-update) | async-done | bytes 524304 | tf_op jit(solution)/shard_map/reduce_scatter | solution.py:66
  789.6 361.7 %reduce-scatter.3.cloned.1.call-done = f32[64,2048]{1,0:T(8,128)} async-done(((f32[2048,2048]{1,0:T(8,128)}), f32[64,2048]{1,0:T(8,128)}) %reduce-scatter.3.cloned.1.call-update) | async-done | bytes 524304 | tf_op jit(solution)/shard_map/reduce_scatter | solution.py:66
  (154 shorter events, 55.0 us)
Async XLA Ops:
  7.2 782.5 %reduce-scatter.5.cloned.1.call-start = ((), (), s32[]{:S(2)}) async-start(), calls=%async_computation.3 | async-start | bytes 17301504 | tf_op jit(solution)/shard_map/reduce_scatter | solution.py:66
  8.9 333.0 %collective-permute-start = (bf16[256,2048]{1,0:T(8,128)(2,1)S(1)}, bf16[256,2048]{1,0:T(8,128)(2,1)}, u32[]{:S(2)}, u32[]{:S(2)}) collective-permute-start(bf16[256,2048]{1,0:T(8,128)(2,1)S(1)} %get-tuple-element.187), channel_id=1, source_target_pairs={{0,2},{2,4},{4,6},{6,8},{8,10},{10,12},{12,14},{14,16},{16,18},{18... | collective-permute-start | bytes 3145736 | tf_op jit(solution)/shard_map/ppermute | solution.py:16
  9.0 332.9 %collective-permute-start.1 = (bf16[256,2048]{1,0:T(8,128)(2,1)S(1)}, bf16[256,2048]{1,0:T(8,128)(2,1)}, u32[]{:S(2)}, u32[]{:S(2)}) collective-permute-start(bf16[256,2048]{1,0:T(8,128)(2,1)S(1)} %get-tuple-element.188), channel_id=1, source_target_pairs={{2,0},{4,2},{6,4},{8,6},{10,8},{12,10},{14,12},{16,14},{18,16},{20... | collective-permute-start | bytes 3145736 | tf_op jit(solution)/shard_map/ppermute | solution.py:18
  12.3 15.6 %copy-start = (f32[1024,1536]{1,0:T(8,128)S(1)}, f32[1024,1536]{1,0:T(8,128)}, u32[]{:S(2)}) copy-start(f32[1024,1536]{1,0:T(8,128)} %get-tuple-element.229) | copy-start | bytes 18874372 | tf_op jit(solution)/shard_map/while
  30.1 2.6 copy-start.1
  32.7 15.6 %copy-start = (f32[1024,1536]{1,0:T(8,128)S(1)}, f32[1024,1536]{1,0:T(8,128)}, u32[]{:S(2)}) copy-start(f32[1024,1536]{1,0:T(8,128)} %get-tuple-element.229) | copy-start | bytes 18874372 | tf_op jit(solution)/shard_map/while
  50.5 2.6 copy-start.1
  53.1 15.6 %copy-start = (f32[1024,1536]{1,0:T(8,128)S(1)}, f32[1024,1536]{1,0:T(8,128)}, u32[]{:S(2)}) copy-start(f32[1024,1536]{1,0:T(8,128)} %get-tuple-element.229) | copy-start | bytes 18874372 | tf_op jit(solution)/shard_map/while
  70.9 2.6 copy-start.1
  73.5 15.6 %copy-start = (f32[1024,1536]{1,0:T(8,128)S(1)}, f32[1024,1536]{1,0:T(8,128)}, u32[]{:S(2)}) copy-start(f32[1024,1536]{1,0:T(8,128)} %get-tuple-element.229) | copy-start | bytes 18874372 | tf_op jit(solution)/shard_map/while
  91.2 2.6 copy-start.1
  93.9 15.6 %copy-start = (f32[1024,1536]{1,0:T(8,128)S(1)}, f32[1024,1536]{1,0:T(8,128)}, u32[]{:S(2)}) copy-start(f32[1024,1536]{1,0:T(8,128)} %get-tuple-element.229) | copy-start | bytes 18874372 | tf_op jit(solution)/shard_map/while
  111.6 2.6 copy-start.1
  114.3 15.6 %copy-start = (f32[1024,1536]{1,0:T(8,128)S(1)}, f32[1024,1536]{1,0:T(8,128)}, u32[]{:S(2)}) copy-start(f32[1024,1536]{1,0:T(8,128)} %get-tuple-element.229) | copy-start | bytes 18874372 | tf_op jit(solution)/shard_map/while
  132.0 2.6 copy-start.1
  134.6 15.6 %copy-start = (f32[1024,1536]{1,0:T(8,128)S(1)}, f32[1024,1536]{1,0:T(8,128)}, u32[]{:S(2)}) copy-start(f32[1024,1536]{1,0:T(8,128)} %get-tuple-element.229) | copy-start | bytes 18874372 | tf_op jit(solution)/shard_map/while
  152.4 2.6 copy-start.1
  155.0 15.6 %copy-start = (f32[1024,1536]{1,0:T(8,128)S(1)}, f32[1024,1536]{1,0:T(8,128)}, u32[]{:S(2)}) copy-start(f32[1024,1536]{1,0:T(8,128)} %get-tuple-element.229) | copy-start | bytes 18874372 | tf_op jit(solution)/shard_map/while
  172.8 2.6 copy-start.1
  175.4 15.6 %copy-start = (f32[1024,1536]{1,0:T(8,128)S(1)}, f32[1024,1536]{1,0:T(8,128)}, u32[]{:S(2)}) copy-start(f32[1024,1536]{1,0:T(8,128)} %get-tuple-element.229) | copy-start | bytes 18874372 | tf_op jit(solution)/shard_map/while
  193.2 2.6 copy-start.1
  195.8 15.6 %copy-start = (f32[1024,1536]{1,0:T(8,128)S(1)}, f32[1024,1536]{1,0:T(8,128)}, u32[]{:S(2)}) copy-start(f32[1024,1536]{1,0:T(8,128)} %get-tuple-element.229) | copy-start | bytes 18874372 | tf_op jit(solution)/shard_map/while
  213.5 2.6 copy-start.1
  216.2 15.6 %copy-start = (f32[1024,1536]{1,0:T(8,128)S(1)}, f32[1024,1536]{1,0:T(8,128)}, u32[]{:S(2)}) copy-start(f32[1024,1536]{1,0:T(8,128)} %get-tuple-element.229) | copy-start | bytes 18874372 | tf_op jit(solution)/shard_map/while
  233.9 2.6 copy-start.1
  236.6 15.6 %copy-start = (f32[1024,1536]{1,0:T(8,128)S(1)}, f32[1024,1536]{1,0:T(8,128)}, u32[]{:S(2)}) copy-start(f32[1024,1536]{1,0:T(8,128)} %get-tuple-element.229) | copy-start | bytes 18874372 | tf_op jit(solution)/shard_map/while
  254.3 2.6 copy-start.1
  256.9 15.6 %copy-start = (f32[1024,1536]{1,0:T(8,128)S(1)}, f32[1024,1536]{1,0:T(8,128)}, u32[]{:S(2)}) copy-start(f32[1024,1536]{1,0:T(8,128)} %get-tuple-element.229) | copy-start | bytes 18874372 | tf_op jit(solution)/shard_map/while
  274.7 2.6 copy-start.1
  277.3 15.6 %copy-start = (f32[1024,1536]{1,0:T(8,128)S(1)}, f32[1024,1536]{1,0:T(8,128)}, u32[]{:S(2)}) copy-start(f32[1024,1536]{1,0:T(8,128)} %get-tuple-element.229) | copy-start | bytes 18874372 | tf_op jit(solution)/shard_map/while
  295.1 2.6 copy-start.1
  297.7 15.6 %copy-start = (f32[1024,1536]{1,0:T(8,128)S(1)}, f32[1024,1536]{1,0:T(8,128)}, u32[]{:S(2)}) copy-start(f32[1024,1536]{1,0:T(8,128)} %get-tuple-element.229) | copy-start | bytes 18874372 | tf_op jit(solution)/shard_map/while
  315.5 2.6 copy-start.1
  318.1 15.6 %copy-start = (f32[1024,1536]{1,0:T(8,128)S(1)}, f32[1024,1536]{1,0:T(8,128)}, u32[]{:S(2)}) copy-start(f32[1024,1536]{1,0:T(8,128)} %get-tuple-element.229) | copy-start | bytes 18874372 | tf_op jit(solution)/shard_map/while
  335.8 2.6 copy-start.1
  338.5 3.3 copy-start.8
  338.5 4.0 copy-start.7
  338.5 13.6 %slice-start.2 = ((s8[8388608]{0:T(1024)(128)(4,1)}), s8[4194304]{0:T(1024)(128)(4,1)S(1)}, s32[]{:S(2)}) async-start(s8[8388608]{0:T(1024)(128)(4,1)} %bitcast.39), calls=%async_computation.6 | async-start | bytes 8388608
  341.8 38.7 %copy-start.4 = (bf16[1024,1536]{1,0:T(8,128)(2,1)}, bf16[1024,1536]{1,0:T(8,128)(2,1)S(1)}, u32[]{:S(2)}) copy-start(bf16[1024,1536]{1,0:T(8,128)(2,1)S(1)} %convert_element_type.84) | copy-start | bytes 9437188
  342.5 9.6 copy-start.9
  342.5 9.6 slice-start.3
  352.1 12.7 %copy-start.12 = (bf16[1024,2048]{1,0:T(8,128)(2,1)}, bf16[1024,2048]{1,0:T(8,128)(2,1)S(1)}, u32[]{:S(2)}) copy-start(bf16[1024,2048]{1,0:T(8,128)(2,1)S(1)} %divide_convert_fusion.3) | copy-start | bytes 12582916
  365.1 15.5 %collective-permute-start.2 = (bf16[256,2048]{1,0:T(8,128)(2,1)S(1)}, bf16[256,2048]{1,0:T(8,128)(2,1)S(1)}, u32[]{:S(2)}, u32[]{:S(2)}) collective-permute-start(bf16[256,2048]{1,0:T(8,128)(2,1)S(1)} %get-tuple-element.185), channel_id=1, source_target_pairs={{0,2},{2,4},{4,6},{6,8},{8,10},{10,12},{12,14},{14,16},{16,18},{18... | collective-permute-start | bytes 3145736 | tf_op jit(solution)/shard_map/ppermute | solution.py:16
  365.3 23.5 %slice-start = ((s8[8388608]{0:T(1024)(128)(4,1)}), s8[4194304]{0:T(1024)(128)(4,1)S(1)}, s32[]{:S(2)}) async-start(s8[8388608]{0:T(1024)(128)(4,1)} %bitcast.37), calls=%async_computation.4 | async-start | bytes 8388608
  365.3 23.5 %slice-start.1 = ((s8[8388608]{0:T(1024)(128)(4,1)}), s8[4194304]{0:T(1024)(128)(4,1)S(1)}, s32[]{:S(2)}) async-start(s8[8388608]{0:T(1024)(128)(4,1)} %bitcast.37), calls=%async_computation.5 | async-start | bytes 8388608
  365.4 23.5 %copy-start.10 = (bf16[1,1024,2048]{2,1,0:T(8,128)(2,1)S(1)}, bf16[1,1024,2048]{2,1,0:T(8,128)(2,1)}, u32[]{:S(2)}) copy-start(bf16[1,1024,2048]{2,1,0:T(8,128)(2,1)} %param.25) | copy-start | bytes 12582916
  365.4 23.5 %copy-start.11 = (f32[2048]{0:T(1024)S(1)}, f32[2048]{0:T(1024)}, u32[]{:S(2)}) copy-start(f32[2048]{0:T(1024)} %param.24) | copy-start | bytes 24580
  365.4 15.2 %collective-permute-start.3 = (bf16[256,2048]{1,0:T(8,128)(2,1)S(1)}, bf16[256,2048]{1,0:T(8,128)(2,1)S(1)}, u32[]{:S(2)}, u32[]{:S(2)}) collective-permute-start(bf16[256,2048]{1,0:T(8,128)(2,1)S(1)} %get-tuple-element.186), channel_id=1, source_target_pairs={{2,0},{4,2},{6,4},{8,6},{10,8},{12,10},{14,12},{16,14},{18,16},{20... | collective-permute-start | bytes 3145736 | tf_op jit(solution)/shard_map/ppermute | solution.py:18
  388.9 20.5 %copy-start.15 = (bf16[1024,2048]{1,0:T(8,128)(2,1)S(1)}, bf16[1024,2048]{1,0:T(8,128)(2,1)}, u32[]{:S(2)}) copy-start(bf16[1024,2048]{1,0:T(8,128)(2,1)} %divide_convert_fusion.2) | copy-start | bytes 12582916
  407.4 2.0 copy-start.14
  420.9 730.4 %reduce-scatter.3.cloned.1.call-start = ((), (), s32[]{:S(2)}) async-start(), calls=%async_computation.2 | async-start | bytes 17301504 | tf_op jit(solution)/shard_map/reduce_scatter | solution.py:66
  421.4 12.7 %copy-start.5 = (bf16[1024,1536]{1,0:T(8,128)(2,1)S(1)}, bf16[1024,1536]{1,0:T(8,128)(2,1)}, u32[]{:S(2)}) copy-start(bf16[1024,1536]{1,0:T(8,128)(2,1)} %copy-done.4) | copy-start | bytes 9437188
  444.7 19.5 %collective-permute-start.4 = (bf16[256,2048]{1,0:T(8,128)(2,1)}, bf16[256,2048]{1,0:T(8,128)(2,1)}, u32[]{:S(2)}, u32[]{:S(2)}) collective-permute-start(bf16[256,2048]{1,0:T(8,128)(2,1)} %get-tuple-element.184), channel_id=1, source_target_pairs={{30,0},{0,2},{2,4},{4,6},{6,8},{8,10},{10,12},{12,14},{14,16},{16,... | collective-permute-start | bytes 3145736 | tf_op jit(solution)/shard_map/ppermute | solution.py:28
  455.7 15.8 %collective-permute-start.5 = (bf16[256,2048]{1,0:T(8,128)(2,1)}, bf16[256,2048]{1,0:T(8,128)(2,1)S(1)}, u32[]{:S(2)}, u32[]{:S(2)}) collective-permute-start(bf16[256,2048]{1,0:T(8,128)(2,1)} %get-tuple-element.183), channel_id=1, source_target_pairs={{2,0},{4,2},{6,4},{8,6},{10,8},{12,10},{14,12},{16,14},{18,16},{20... | collective-permute-start | bytes 3145736 | tf_op jit(solution)/shard_map/ppermute | solution.py:28
  472.0 10.5 copy-start.13
  480.5 2.0 copy-start.3
  494.2 12.8 %copy-start.6 = (bf16[1024,1536]{1,0:T(8,128)(2,1)S(1)}, bf16[1024,1536]{1,0:T(8,128)(2,1)}, u32[]{:S(2)}) copy-start(bf16[1024,1536]{1,0:T(8,128)(2,1)} %copy-done.4) | copy-start | bytes 9437188
  507.0 9.1 copy-start.2
  517.3 82.5 %collective-permute-start.6 = (bf16[256,2048]{1,0:T(8,128)(2,1)}, bf16[256,2048]{1,0:T(8,128)(2,1)S(1)}, u32[]{:S(2)}, u32[]{:S(2)}) collective-permute-start(bf16[256,2048]{1,0:T(8,128)(2,1)} %get-tuple-element.182), channel_id=1, source_target_pairs={{30,0},{0,2},{2,4},{4,6},{6,8},{8,10},{10,12},{12,14},{14,16},{16,... | collective-permute-start | bytes 3145736 | tf_op jit(solution)/shard_map/ppermute | solution.py:28
  534.2 68.9 %collective-permute-start.7 = (bf16[256,2048]{1,0:T(8,128)(2,1)S(1)}, bf16[256,2048]{1,0:T(8,128)(2,1)S(1)}, u32[]{:S(2)}, u32[]{:S(2)}) collective-permute-start(bf16[256,2048]{1,0:T(8,128)(2,1)S(1)} %get-tuple-element.181), channel_id=1, source_target_pairs={{2,0},{4,2},{6,4},{8,6},{10,8},{12,10},{14,12},{16,14},{18,16},{20... | collective-permute-start | bytes 3145736 | tf_op jit(solution)/shard_map/ppermute | solution.py:28
Sparse Core Ops, SparseCore 0:
  421.0 368.5 reduce-scatter.4
  792.5 358.8 reduce-scatter.2
where the time goes:
time: 1170 us; the launch traced here: 1160 us
  waiting for transfers between devices  561 us (48%)
  other arithmetic  311 us (27%)
  matrix products  116 us (10%)
  local copies, waits for them, and re-layouts  67.3 us (6%)
  blocking collectives  54.3 us (5%)
  starting transfers between devices  34 us (3%)
  between operations  14.5 us (1%)
    reduce_scatter x2, waiting for transfers between devices, reduce_grads(): lax.psum_scatter(grad_weight, ('blk', 'grp'), scatter_dimension=0, tiled=...  539 us
    reduce_sum x16, other arithmetic, add_block(): return counts + jnp.sum(match * block_used[:, :, None], axis=1)  234 us
    unnamed x1, blocking collectives  54.3 us
    while x64, local copies, waits for them, and re-layouts  42 us
    add x16, other arithmetic, add_block(): return counts + jnp.sum(match * block_used[:, :, None], axis=1)  34.4 us
    dot_general x2, matrix products, aggregate(): jnp.dot(averaged, weight, preferred_element_type=jnp.float32) + bias_vec  31.2 us
    ppermute x4, starting transfers between devices, passed_along(): return lax.ppermute(block, axis, route)  27.9 us
    dot_general x2, matrix products, layer_back(): lax.dot_general(grad_pre, weight, (((1,), (1,)), ((), ())), preferred_ele...  25.5 us
  transfers between devices with their start and end apart: 10, of which 5 were waited for; matrix products, arithmetic and copies ran while one was open for 33% of the time, Pallas kernels for 0%

commit v1 on v0

v1 whole, which is shorter than its diff:
```python
import jax
import jax.numpy as jnp
from jax import lax
from jax.experimental import pallas as pl
from jax.experimental.pallas import tpu as pltpu
from jax.sharding import PartitionSpec as P

BAND = 256
BF = jnp.bfloat16
F32 = jnp.float32


def count_kernel(slots_ref, degree_ref, out_ref):
    slot_total, lanes = slots_ref.shape
    width = out_ref.shape[0]
    quarter = width // 4
    parts = 2
    rows = quarter // parts
    degree = degree_ref[...]
    block = pl.program_id(0)
    node = lax.broadcasted_iota(jnp.int32, (rows, lanes), 1) + block * lanes
    sub = lax.broadcasted_iota(jnp.int32, (rows, lanes), 0)
    for part in range(parts):
        ids = sub + part * rows

        def add_slot(k, packed):
            slot = slots_ref[pl.ds(k, 1), :]
            q = (
                (slot >= quarter).astype(jnp.int32)
                + (slot >= 2 * quarter).astype(jnp.int32)
                + (slot >= 3 * quarter).astype(jnp.int32)
            )
            key = slot - q * quarter
            value = jnp.where(k < degree, jnp.left_shift(1, q * 8), 0)
            return packed + jnp.where(ids == key, value, 0)

        packed = lax.fori_loop(
            0, slot_total, add_slot, jnp.zeros((rows, lanes), jnp.int32), unroll=4
        )
        for q in range(4):
            count = jnp.bitwise_and(jnp.right_shift(packed, 8 * q), 255)
            own = ids + (q * quarter - BAND) == node
            count = count + jnp.where(own, 2, 0)
            out_ref[pl.ds(q * quarter + part * rows, rows), :] = count.astype(F32).astype(BF)


def count_table(slots, degree):
    nodes, slot_total = slots.shape
    width = nodes + 2 * BAND
    return pl.pallas_call(
        count_kernel,
        grid=(nodes // 128,),
        in_specs=[
            pl.BlockSpec((slot_total, 128), lambda i: (0, i)),
            pl.BlockSpec((1, 128), lambda i: (0, i)),
        ],
        out_specs=pl.BlockSpec((width, 128), lambda i: (0, i)),
        out_shape=jax.ShapeDtypeStruct((width, nodes), BF),
        cost_estimate=pl.CostEstimate(flops=0, bytes_accessed=4 << 20, transcendentals=0),
    )(slots.T, degree[None, :])


def dot(a, b, contract):
    return lax.dot_general(a, b, (contract, ((), ())), preferred_element_type=F32)


def halo(field):
    count = lax.axis_size("blk")
    nodes = field.shape[0]
    before = lax.ppermute(field[nodes - BAND :], "blk", [(i, (i + 1) % count) for i in range(count)])
    after = lax.ppermute(field[:BAND], "blk", [((i + 1) % count, i) for i in range(count)])
    return before, after


def aggregate(field, table, degree_plus, weight, bias_vec):
    before, after = halo(field)
    window = jnp.concatenate([before, field, after], axis=0)
    pre_sum = dot(table, window, ((0,), (0,)))
    averaged = (pre_sum / degree_plus).astype(BF)
    preact = dot(averaged, weight, ((1,), (0,))) + bias_vec
    return averaged, preact


def swap_half(total, dim, bit, partner, axis):
    size = total.shape[dim] // 2
    send = lax.dynamic_slice_in_dim(total, (1 - bit) * size, size, dim)
    keep = lax.dynamic_slice_in_dim(total, bit * size, size, dim)
    received = lax.ppermute(send.astype(BF), axis, partner)
    return keep + received.astype(F32)


def line_sum(total, place, count, step_perm):
    mine = lax.dynamic_index_in_dim(total, place, 0, keepdims=False)
    below = None
    above = None
    for step in range(1, count):
        def part(index, carried):
            chunk = lax.dynamic_index_in_dim(total, jnp.clip(index, 0, count - 1), 0, keepdims=False)
            return chunk if carried is None else chunk + carried.astype(F32)

        up = part(place + count - step, below).astype(BF)
        down = part(place - count + step, above).astype(BF)
        below = lax.ppermute(up, "blk", step_perm([(z, z + 1) for z in range(step)]))
        above = lax.ppermute(
            down, "blk", step_perm([(z, z - 1) for z in range(count - step, count)])
        )
    return mine + below.astype(F32) + above.astype(F32)


def scatter_sum(averaged, grad_pre):
    blk, grp = lax.axis_size("blk"), lax.axis_size("grp")
    b, g = lax.axis_index("blk"), lax.axis_index("grp")
    core, y, z = b % 2, (b // 2) % 2, b // 4
    line = blk // 4
    nodes, width = averaged.shape
    rows = width // (blk * grp)

    def step_perm(pairs):
        return [(4 * s + r, 4 * t + r) for s, t in pairs for r in range(4)]

    by_core = averaged.reshape(nodes, blk // 2, 2, grp * rows)

    def half(which):
        return lax.dynamic_index_in_dim(by_core, which, 2, keepdims=False).reshape(nodes, width // 2)

    send = dot(half(1 - core), grad_pre, ((0,), (0,))).astype(BF)
    received = lax.ppermute(send, "blk", [(i, i ^ 1) for i in range(blk)])
    total = dot(half(core), grad_pre, ((0,), (0,))) + received.astype(F32)
    total = total.reshape(line, 2, grp, rows, width)
    span = grp
    while span > 1:
        span //= 2
        total = swap_half(total, 2, (g // span) % 2, [(i, i ^ span) for i in range(grp)], "grp")
    total = total[:, :, 0]
    total = line_sum(total, z, line, step_perm)
    total = swap_half(total, 0, y, [(i, i ^ 2) for i in range(blk)], "blk")
    return total[0]


def layer_back(grad_out, preact, averaged, table, degree_plus, weight):
    nodes = averaged.shape[0]
    blk = lax.axis_size("blk")
    _, gelu_pull = jax.vjp(jax.nn.gelu, preact)
    grad_pre = gelu_pull(grad_out)[0].astype(BF)
    grad_weight = scatter_sum(averaged, grad_pre)
    grad_bias = lax.psum_scatter(
        jnp.sum(grad_pre.astype(F32), axis=0), ("blk", "grp"), scatter_dimension=0, tiled=True
    )
    grad_avg = dot(grad_pre, weight, ((1,), (1,)))
    grad_scaled = (grad_avg / degree_plus).astype(BF)
    grad_window = dot(table, grad_scaled, ((1,), (0,)))
    from_next = lax.ppermute(
        grad_window[:BAND].astype(BF), "blk", [((i + 1) % blk, i) for i in range(blk)]
    ).astype(F32)
    from_prev = lax.ppermute(
        grad_window[BAND + nodes :].astype(BF), "blk", [(i, (i + 1) % blk) for i in range(blk)]
    ).astype(F32)
    own = grad_window[BAND : BAND + nodes]
    grad_in = jnp.concatenate(
        [own[:BAND] + from_prev, own[BAND : nodes - BAND], own[nodes - BAND :] + from_next]
    )
    return grad_in, grad_weight, grad_bias


def local(features, neighbours, degree, weight_one, bias_one, weight_two, bias_two, cotangent):
    table = count_table(neighbours[0], degree[0])
    degree_plus = degree[0].astype(F32)[:, None] + 1.0
    averaged_one, preact_one = aggregate(features[0], table, degree_plus, weight_one, bias_one)
    hidden = jax.nn.gelu(preact_one).astype(BF)
    averaged_two, preact_two = aggregate(hidden, table, degree_plus, weight_two, bias_two)
    activations = jax.nn.gelu(preact_two).astype(BF)
    grad_hidden, grad_w_two, grad_b_two = layer_back(
        cotangent[0].astype(F32), preact_two, averaged_two, table, degree_plus, weight_two
    )
    grad_input, grad_w_one, grad_b_one = layer_back(
        grad_hidden, preact_one, averaged_one, table, degree_plus, weight_one
    )
    return (
        activations[None],
        grad_input.astype(BF)[None],
        grad_w_one,
        grad_b_one,
        grad_w_two,
        grad_b_two,
    )


def solution(mesh):
    rows = P("grp", "blk", None)
    spread = ("blk", "grp")
    return jax.shard_map(
        local,
        mesh=mesh,
        in_specs=(rows, rows, P("grp", "blk"), P(), P(), P(), P(), rows),
        out_specs=(rows, rows, P(spread, None), P(spread), P(spread, None), P(spread)),
        check_vma=False,
    )
```

time: 1170 us -> 464 us (0.40)
  waiting for transfers between devices: 561 us -> 84 us
  other arithmetic: 311 us -> 28.8 us
  local copies, waits for them, and re-layouts: 67.3 us -> 105 us
  Pallas kernels: 0 us -> 21 us
  matrix products: 116 us -> 134 us
  between operations: 14.5 us -> 1.64 us
    reduce_scatter x2 -> x0, waiting for transfers between devices: 539 us -> none  [reduce_grads(): lax.psum_scatter(grad_weight, ('blk', 'grp'), scatter_dimension=0, tiled=...]
    reduce_sum x17 -> x1, other arithmetic: 243 us -> 6.3 us  [layer_back(): jnp.sum(grad_pre.astype(F32), axis=0)]
    ppermute x8 -> x26, waiting for transfers between devices: 21.9 us -> 84 us  [the longest x4 49 us: swap_half(): received = lax.ppermute(send.astype(BF), axis, partner)]
    unnamed x38 -> x48, local copies, waits for them, and re-layouts: 5.84 us -> 52.1 us
    while x64 -> x0, local copies, waits for them, and re-layouts: 42 us -> none
    add x19 -> x6, other arithmetic: 49.2 us -> 9.82 us  [the longest x2 5.91 us: swap_half(): return keep + received.astype(F32)]
    pallas_call x0 -> x1, Pallas kernels: none -> 21 us  [count_table(): pl.pallas_call(count_kernel, grid=(nodes // 128,), in_specs=[pl.BlockSpec...]
    dot_general x10, matrix products: 116 us -> 134 us  [dot(): lax.dot_general(a, b, (contract, ((), ())), preferred_element_type=F32)]
  transfers between devices with their start and end apart: 10 -> 26, of which waited for: 5 -> 7; matrix products, arithmetic and copies ran while one was open for 33% -> 36% of each run, Pallas kernels for 0% -> 5%
where the time goes in v1:
time: 464 us; the launch traced here: 456 us
  matrix products  134 us (29%)
  local copies, waits for them, and re-layouts  105 us (23%)
  waiting for transfers between devices  84 us (18%)
  blocking collectives  44 us (9%)
  starting transfers between devices  37.4 us (8%)
  other arithmetic  28.8 us (6%)
  Pallas kernels  21 us (5%)
    dot_general x10, matrix products, dot(): lax.dot_general(a, b, (contract, ((), ())), preferred_element_type=F32)  134 us
    unnamed x48, local copies, waits for them, and re-layouts  52.1 us
    ppermute x4, waiting for transfers between devices, swap_half(): received = lax.ppermute(send.astype(BF), axis, partner)  49 us
    unnamed x1, blocking collectives  44 us
    ppermute x6, waiting for transfers between devices, line_sum(): lax.ppermute(down, 'blk', step_perm([(z, z - 1) for z in range(count - st...  34.9 us
    dynamic_slice x2, local copies, waits for them, and re-layouts, half(): lax.dynamic_index_in_dim(by_core, which, 2, keepdims=False)  21.3 us
    pallas_call x1, Pallas kernels, count_table(): pl.pallas_call(count_kernel, grid=(nodes // 128,), in_specs=[pl.BlockSpec...  21 us
    reshape x2, local copies, waits for them, and re-layouts, scatter_sum(): by_core = averaged.reshape(nodes, blk // 2, 2, grp * rows)  15.5 us
  transfers between devices with their start and end apart: 26, of which 7 were waited for; matrix products, arithmetic and copies ran while one was open for 36% of the time, Pallas kernels for 5%

profile of v1, /device:TPU:18, one launch (start us, length us, event | category | flops | bytes accessed | tf_op | source)
XLA Modules:
  0.0 456.4 jit_solution(7360580272289589359)
XLA Ops:
  0.6 1.7 slice_bitcast_fusion.2
  2.4 2.6 collective-permute-start.1
  5.0 21.0 %shard_map.127 = bf16[1536,1024]{1,0:T(8,128)(2,1)} custom-call(s32[64,1024]{1,0:T(8,128)} %bitcast.118, s32[1,1024]{1,0:T(1,128)} %degree_ref.1), custom_call_target="tpu_custom_call" | custom-call | bytes 4194304 | tf_op jit(solution)/shard_map/pallas_call | solution.py:50
  26.1 9.8 %divide_convert_fusion.3 = bf16[1024,2048]{1,0:T(8,128)(2,1)S(1)} fusion(f32[1024]{0:T(1024)S(1)} %bitcast.119, bf16[1536,1024]{1,0:T(8,128)(2,1)} %shard_map.127, bf16[256,2048]{1,0:T(8,128)(2,1)} %collective-permute-done.1, bf16[1024,2048]{1,0:T(8,128)(2,1)} %bitcast.117, bf16[256,2048]{1,0:T(8,128)(2,1)S(1)} %collective-permute-done), kind=kOutput, calls=%fused_computation.33 | convolution fusion | flops 6465519616 | bytes 13635584 | tf_op jit(solution)/shard_map/dot_general | solution.py:64
  35.9 16.3 %multiply_convert_fusion.1 = (bf16[1024,2048]{1,0:T(8,128)(2,1)S(1)}, f32[1024,2048]{1,0:T(8,128)}) fusion(f32[2048]{0:T(1024)S(1)} %copy-done.17, bf16[1024,2048]{1,0:T(8,128)(2,1)S(1)} %divide_convert_fusion.3, bf16[2048,2048]{1,0:T(8,128)(2,1)} %param.11), kind=kOutput, calls=%fused_computation.32 | convolution fusion | flops 8610906112 | bytes 25174016 | tf_op jit(solution)/shard_map/dot_general | solution.py:64
  52.2 2.0 copy-done.15
  54.2 1.6 fusion.66
  55.8 2.6 collective-permute-start.2
  58.6 7.8 %reshape.133 = bf16[1024,8,2,128]{3,2,1,0:T(2,128)(2,1)} reshape(bf16[1024,2048]{1,0:T(8,128)(2,1)} %copy-done.8) | data formatting | bytes 8388608 | tf_op jit(solution)/shard_map/reshape | solution.py:121
  66.4 11.2 %constant_dynamic-slice_fusion.2 = (bf16[1024,8,1,128]{3,2,1,0:T(2,128)(2,1)}, bf16[1024,8,1,128]{3,2,1,0:T(2,128)(2,1)}) fusion(bf16[1024,8,2,128]{3,2,1,0:T(2,128)(2,1)} %reshape.133, s32[]{:T(128)S(6)} %select_n.76, s32[]{:T(128)S(6)} %select_n.75), kind=kLoop, calls=%fused_computation.105 | loop fusion | bytes 8388616 | tf_op jit(solution)/shard_map/jit(dynamic_index_in_dim)/dynamic_slice | solution.py:124
  77.6 10.7 %copy.35 = bf16[1024,8,1,128]{0,3,1,2:T(8,128)(2,1)} copy(bf16[1024,8,1,128]{3,2,1,0:T(2,128)(2,1)} %get-tuple-element.31) | data formatting | bytes 4194304
  88.3 10.3 %divide_convert_fusion.2 = bf16[1024,2048]{1,0:T(8,128)(2,1)} fusion(f32[1024]{0:T(1024)S(1)} %bitcast.120, bf16[1536,1024]{1,0:T(8,128)(2,1)S(1)} %copy-done.11, bf16[256,2048]{1,0:T(8,128)(2,1)} %collective-permute-done.3, bf16[1024,2048]{1,0:T(8,128)(2,1)} %copy-done.15, bf16[256,2048]{1,0:T(8,128)(2,1)} %collective-permute-done.2), kind=kOutput, calls=%fused_computation.31 | convolution fusion | flops 6465519616 | bytes 13635584 | tf_op jit(solution)/shard_map/dot_general | solution.py:64
  98.6 7.7 %reshape.137 = bf16[1024,8,2,128]{3,2,1,0:T(2,128)(2,1)} reshape(bf16[1024,2048]{1,0:T(8,128)(2,1)} %divide_convert_fusion.2) | data formatting | bytes 8388608 | tf_op jit(solution)/shard_map/reshape | solution.py:121
  106.3 21.0 %convert_reduce_fusion = (f32[2048]{0:T(1024)S(1)}, bf16[1024,2048]{1,0:T(8,128)(2,1)}, bf16[1,1024,2048]{2,1,0:T(8,128)(2,1)}) fusion(f32[2048]{0:T(1024)S(1)} %copy-done.18, bf16[1,1024,2048]{2,1,0:T(8,128)(2,1)} %param.15, bf16[1024,2048]{1,0:T(8,128)(2,1)} %divide_convert_fusion.2, bf16[2048,2048]{1,0:T(8,128)(2,1)} %param.13), kind=kOutput, calls=%fused_computation.24 | convolution fusion | flops 8644458496 | bytes 25182208 | tf_op jit(solution)/shard_map/dot_general | solution.py:64
  127.4 23.2 %fusion.67 = (bf16[1536,2048]{1,0:T(8,128)(2,1)}, f32[1536,2048]{1,0:T(8,128)}) fusion(bf16[1536,1024]{1,0:T(8,128)(2,1)S(1)} %copy-done.11, bf16[1024,2048]{1,0:T(8,128)(2,1)} %get-tuple-element.9, bf16[2048,2048]{1,0:T(8,128)(2,1)} %param.13, f32[1024]{0:T(1024)S(1)} %bitcast.121), kind=kOutput, calls=%fused_computation.113 | convolution fusion | flops 15039725568 | bytes 34607104 | tf_op jit(solution)/shard_map/dot_general | solution.py:64
  150.6 3.3 fusion.65
  154.7 1.8 collective-permute-start.5
  156.5 10.1 %constant_dynamic-slice_fusion = (bf16[1024,8,1,128]{3,2,1,0:T(2,128)(2,1)}, bf16[1024,8,1,128]{3,2,1,0:T(2,128)(2,1)}) fusion(bf16[1024,8,2,128]{3,2,1,0:T(2,128)(2,1)S(1)} %copy-done, s32[]{:T(128)S(6)} %select_n.76, s32[]{:T(128)S(6)} %select_n.75), kind=kLoop, calls=%fused_computation.103 | loop fusion | bytes 8388616 | tf_op jit(solution)/shard_map/jit(dynamic_index_in_dim)/dynamic_slice | solution.py:124
  166.6 10.6 %copy.39 = bf16[1024,8,1,128]{0,3,1,2:T(8,128)(2,1)} copy(bf16[1024,8,1,128]{3,2,1,0:T(2,128)(2,1)} %get-tuple-element.25) | data formatting | bytes 4194304
  177.1 9.3 %convolution_convert_fusion = bf16[1024,2048]{1,0:T(8,128)(2,1)} fusion(bf16[1024,1024]{0,1:T(8,128)(2,1)} %bitcast.116, bf16[1024,2048]{1,0:T(8,128)(2,1)} %get-tuple-element.9), kind=kOutput, calls=%fused_computation.58 | convolution fusion | flops 4297064448 | bytes 10485760 | tf_op jit(solution)/shard_map/dot_general | solution.py:64
  186.5 2.8 slice.81
  189.3 3.6 slice_add_fusion.3
  193.5 6.3 %convert_reduce_fusion.1 = (f32[2048]{0:T(1024)S(1)}, bf16[1024,2048]{1,0:T(8,128)(2,1)S(1)}) fusion(f32[1024,2048]{1,0:T(8,128)S(1)} %bitcast.108, f32[2048]{0:T(1024)S(1)} %copy-done.17, f32[256,2048]{1,0:T(8,128)S(1)} %get-tuple-element.15, f32[512,2048]{1,0:T(8,128)S(1)} %slice.81, f32[256,2048]{1,0:T(8,128)S(1)} %get-tuple-element.14), kind=kLoop, calls=%fused_computation.26 | loop fusion | flops 52426752 | bytes 20987904 | tf_op jit(solution)/shard_map/reduce_sum | solution.py:147
  199.8 6.1 %convolution_convert_fusion.1 = bf16[1024,2048]{1,0:T(8,128)(2,1)} fusion(bf16[1024,1024]{0,1:T(8,128)(2,1)S(1)} %bitcast.113, bf16[1024,2048]{1,0:T(8,128)(2,1)S(1)} %get-tuple-element.11), kind=kOutput, calls=%fused_computation.59 | convolution fusion | flops 4297064448 | bytes 10485760 | tf_op jit(solution)/shard_map/dot_general | solution.py:64
  206.5 10.5 %copy.34 = bf16[1024,8,1,128]{0,3,1,2:T(8,128)(2,1)} copy(bf16[1024,8,1,128]{3,2,1,0:T(2,128)(2,1)} %get-tuple-element.32) | data formatting | bytes 4194304
  217.0 10.7 %copy.38 = bf16[1024,8,1,128]{0,3,1,2:T(8,128)(2,1)} copy(bf16[1024,8,1,128]{3,2,1,0:T(2,128)(2,1)} %get-tuple-element.26) | data formatting | bytes 4194304
  227.8 8.7 %convert_add_fusion = f32[1024,2048]{1,0:T(8,128)S(1)} fusion(bf16[1024,2048]{1,0:T(8,128)(2,1)} %collective-permute-done.17, bf16[1024,1024]{0,1:T(8,128)(2,1)} %bitcast.115, bf16[1024,2048]{1,0:T(8,128)(2,1)} %get-tuple-element.9), kind=kOutput, calls=%fused_computation.25 | convolution fusion | flops 4299161600 | bytes 18874368 | tf_op jit(solution)/shard_map/dot_general | solution.py:64
  236.5 2.0 bitcast_convert_fusion
  239.0 1.4 copy-done.7
  240.5 6.3 %convert_add_fusion.1 = f32[1024,2048]{1,0:T(8,128)S(1)} fusion(bf16[1024,2048]{1,0:T(8,128)(2,1)} %collective-permute-done.8, bf16[1024,1024]{0,1:T(8,128)(2,1)S(1)} %bitcast.114, bf16[1024,2048]{1,0:T(8,128)(2,1)S(1)} %copy-done.10), kind=kOutput, calls=%fused_computation.27 | convolution fusion | flops 4299161600 | bytes 18874368 | tf_op jit(solution)/shard_map/dot_general | solution.py:64
  246.8 3.2 copy-done.5
  250.0 1.6 bitcast_convert_fusion.1
  252.2 23.0 %fusion.68 = (bf16[1536,2048]{1,0:T(8,128)(2,1)}, f32[1536,2048]{1,0:T(8,128)}) fusion(bf16[1536,1024]{1,0:T(8,128)(2,1)S(1)} %copy-done.11, bf16[1024,2048]{1,0:T(8,128)(2,1)} %copy-done.9, bf16[2048,2048]{1,0:T(8,128)(2,1)} %param.11, f32[1024]{0:T(1024)S(1)} %bitcast.122), kind=kOutput, calls=%fused_computation.114 | convolution fusion | flops 15039725568 | bytes 34607104 | tf_op jit(solution)/shard_map/dot_general | solution.py:64
  275.2 12.1 %collective-permute-done.18 = bf16[4,2,1,64,2048]{4,3,1,2,0:T(8,128)(2,1)} collective-permute-done((bf16[4,2,1,64,2048]{4,3,1,2,0:T(8,128)(2,1)}, bf16[4,2,1,64,2048]{4,3,1,2,0:T(8,128)(2,1)}, u32[]{:S(2)}, u32[]{:S(2)}) %collective-permute-start.18) | collective-permute-done | bytes 2097184 | tf_op jit(solution)/shard_map/ppermute | solution.py:88
  287.3 3.4 bitcast_add_fusion
  290.7 0.9 fusion.58
  292.5 1.2 fusion.64
  293.7 2.6 collective-permute-start.7
  296.3 1.3 collective-permute-start.22
  297.6 0.9 fusion.48
  298.5 1.3 collective-permute-start.20
  299.8 31.5 %collective-permute-done.9 = bf16[4,2,1,64,2048]{4,3,1,2,0:T(8,128)(2,1)} collective-permute-done((bf16[4,2,1,64,2048]{4,3,1,2,0:T(8,128)(2,1)}, bf16[4,2,1,64,2048]{4,3,1,2,0:T(8,128)(2,1)}, u32[]{:S(2)}, u32[]{:S(2)}) %collective-permute-start.9) | collective-permute-done | bytes 2097184 | tf_op jit(solution)/shard_map/ppermute | solution.py:88
  331.3 2.5 bitcast_add_fusion.1
  333.8 1.3 fusion.56
  335.1 1.1 copy-done.3
  336.1 1.4 collective-permute-start.10
  337.7 44.0 %all-reduce.2 = (f32[2048]{0:T(1024)S(1)}, f32[2048]{0:T(1024)S(1)}) all-reduce(f32[2048]{0:T(1024)S(1)} %get-tuple-element.10, f32[2048]{0:T(1024)S(1)} %get-tuple-element.8), channel_id=2, replica_groups=mesh['blk'=16,'grp'=2] {'blk','grp'}, use_global_device_ids=true, to_apply=%region_1.2.clone | all-reduce | flops 4096 | bytes 32768
  382.9 2.1 fusion.49
  385.0 3.5 collective-permute-start.23
  388.6 1.3 collective-permute-start.13
  389.9 1.5 fusion.53
  391.4 1.3 collective-permute-start.11
  392.7 3.7 fusion.44
  396.4 4.0 collective-permute-start.21
  400.4 11.2 %collective-permute-done.13 = bf16[2,64,2048]{2,1,0:T(8,128)(2,1)S(1)} collective-permute-done((bf16[2,64,2048]{2,1,0:T(8,128)(2,1)}, bf16[2,64,2048]{2,1,0:T(8,128)(2,1)S(1)}, u32[]{:S(2)}, u32[]{:S(2)}) %collective-permute-start.13) | collective-permute-done | bytes 524320 | tf_op jit(solution)/shard_map/ppermute | solution.py:104
  411.8 1.9 collective-permute-start.14
  413.9 1.9 collective-permute-start.24
  415.8 2.3 pad_maximum_fusion.1
  418.1 3.9 collective-permute-start.12
  422.1 6.5 %collective-permute-done.14 = bf16[2,64,2048]{2,1,0:T(8,128)(2,1)S(1)} collective-permute-done((bf16[2,64,2048]{2,1,0:T(8,128)(2,1)S(1)}, bf16[2,64,2048]{2,1,0:T(8,128)(2,1)S(1)}, u32[]{:S(2)}, u32[]{:S(2)}) %collective-permute-start.14) | collective-permute-done | bytes 524320 | tf_op jit(solution)/shard_map/ppermute | solution.py:104
  428.7 1.9 collective-permute-start.15
  430.6 9.2 %collective-permute-done.24 = bf16[2,64,2048]{2,1,0:T(8,128)(2,1)S(1)} collective-permute-done((bf16[2,64,2048]{2,1,0:T(8,128)(2,1)S(1)}, bf16[2,64,2048]{2,1,0:T(8,128)(2,1)S(1)}, u32[]{:S(2)}, u32[]{:S(2)}) %collective-permute-start.24) | collective-permute-done | bytes 524320 | tf_op jit(solution)/shard_map/ppermute | solution.py:104
  440.4 8.0 %collective-permute-done.15 = bf16[2,64,2048]{2,1,0:T(8,128)(2,1)S(1)} collective-permute-done((bf16[2,64,2048]{2,1,0:T(8,128)(2,1)S(1)}, bf16[2,64,2048]{2,1,0:T(8,128)(2,1)S(1)}, u32[]{:S(2)}, u32[]{:S(2)}) %collective-permute-start.15) | collective-permute-done | bytes 524320 | tf_op jit(solution)/shard_map/ppermute | solution.py:104
  449.6 5.5 %collective-permute-done.16 = bf16[1,64,2048]{2,1,0:T(8,128)(2,1)S(1)} collective-permute-done((bf16[1,64,2048]{2,1,0:T(8,128)(2,1)S(1)}, bf16[1,64,2048]{2,1,0:T(8,128)(2,1)S(1)}, u32[]{:S(2)}, u32[]{:S(2)}) %collective-permute-start.16) | collective-permute-done | bytes 262176 | tf_op jit(solution)/shard_map/ppermute | solution.py:88
  (82 shorter events, 8.6 us)
Async XLA Ops:
  0.6 25.4 %copy-start.16 = (s32[1,1024]{1,0:T(1,128)S(1)}, s32[1,1024]{1,0:T(1,128)}, u32[]{:S(2)}) copy-start(s32[1,1024]{1,0:T(1,128)} %degree_ref.1) | copy-start | bytes 12292
  2.3 23.7 %collective-permute-start = (bf16[256,2048]{1,0:T(8,128)(2,1)S(1)}, bf16[256,2048]{1,0:T(8,128)(2,1)S(1)}, u32[]{:S(2)}, u32[]{:S(2)}) collective-permute-start(bf16[256,2048]{1,0:T(8,128)(2,1)S(1)} %get-tuple-element.35), channel_id=1, source_target_pairs={{0,2},{2,4},{4,6},{6,8},{8,10},{10,12},{12,14},{14,16},{16,18},{18... | collective-permute-start | bytes 3145736 | tf_op jit(solution)/shard_map/ppermute | solution.py:70
  2.4 23.7 %collective-permute-start.1 = (bf16[256,2048]{1,0:T(8,128)(2,1)S(1)}, bf16[256,2048]{1,0:T(8,128)(2,1)}, u32[]{:S(2)}, u32[]{:S(2)}) collective-permute-start(bf16[256,2048]{1,0:T(8,128)(2,1)S(1)} %get-tuple-element.36), channel_id=1, source_target_pairs={{2,0},{4,2},{6,4},{8,6},{10,8},{12,10},{14,12},{16,14},{18,16},{20... | collective-permute-start | bytes 3145736 | tf_op jit(solution)/shard_map/ppermute | solution.py:71
  26.1 9.8 %copy-start.17 = (f32[2048]{0:T(1024)S(1)}, f32[2048]{0:T(1024)}, u32[]{:S(2)}) copy-start(f32[2048]{0:T(1024)} %param.12) | copy-start | bytes 24580
  35.9 16.3 %copy-start.8 = (bf16[1024,2048]{1,0:T(8,128)(2,1)}, bf16[1024,2048]{1,0:T(8,128)(2,1)S(1)}, u32[]{:S(2)}) copy-start(bf16[1024,2048]{1,0:T(8,128)(2,1)S(1)} %divide_convert_fusion.3) | copy-start | bytes 12582916
  52.2 2.0 copy-start.15
  55.8 32.5 %collective-permute-start.2 = (bf16[256,2048]{1,0:T(8,128)(2,1)}, bf16[256,2048]{1,0:T(8,128)(2,1)}, u32[]{:S(2)}, u32[]{:S(2)}) collective-permute-start(bf16[256,2048]{1,0:T(8,128)(2,1)} %get-tuple-element.33), channel_id=1, source_target_pairs={{0,2},{2,4},{4,6},{6,8},{8,10},{10,12},{12,14},{14,16},{16,18},{18... | collective-permute-start | bytes 3145736 | tf_op jit(solution)/shard_map/ppermute | solution.py:70
  58.3 29.9 %collective-permute-start.3 = (bf16[256,2048]{1,0:T(8,128)(2,1)}, bf16[256,2048]{1,0:T(8,128)(2,1)}, u32[]{:S(2)}, u32[]{:S(2)}) collective-permute-start(bf16[256,2048]{1,0:T(8,128)(2,1)} %get-tuple-element.34), channel_id=1, source_target_pairs={{2,0},{4,2},{6,4},{8,6},{10,8},{12,10},{14,12},{16,14},{18,16},{20... | collective-permute-start | bytes 3145736 | tf_op jit(solution)/shard_map/ppermute | solution.py:71
  77.6 10.7 %copy-start.11 = (bf16[1536,1024]{1,0:T(8,128)(2,1)S(1)}, bf16[1536,1024]{1,0:T(8,128)(2,1)}, u32[]{:S(2)}) copy-start(bf16[1536,1024]{1,0:T(8,128)(2,1)} %shard_map.127) | copy-start | bytes 9437188
  98.6 7.7 %copy-start.18 = (f32[2048]{0:T(1024)S(1)}, f32[2048]{0:T(1024)}, u32[]{:S(2)}) copy-start(f32[2048]{0:T(1024)} %param.14) | copy-start | bytes 24580
  150.6 6.0 %copy-start = (bf16[1024,8,2,128]{3,2,1,0:T(2,128)(2,1)S(1)}, bf16[1024,8,2,128]{3,2,1,0:T(2,128)(2,1)}, u32[]{:S(2)}) copy-start(bf16[1024,8,2,128]{3,2,1,0:T(2,128)(2,1)} %reshape.137) | copy-start | bytes 12582916
  153.9 35.4 %collective-permute-start.4 = (bf16[256,2048]{1,0:T(8,128)(2,1)}, bf16[256,2048]{1,0:T(8,128)(2,1)}, u32[]{:S(2)}, u32[]{:S(2)}) collective-permute-start(bf16[256,2048]{1,0:T(8,128)(2,1)} %get-tuple-element.19), channel_id=1, source_target_pairs={{0,2},{2,4},{4,6},{6,8},{8,10},{10,12},{12,14},{14,16},{16,18},{18... | collective-permute-start | bytes 3145736 | tf_op jit(solution)/shard_map/ppermute | solution.py:155
  154.7 34.6 %collective-permute-start.5 = (bf16[256,2048]{1,0:T(8,128)(2,1)}, bf16[256,2048]{1,0:T(8,128)(2,1)}, u32[]{:S(2)}, u32[]{:S(2)}) collective-permute-start(bf16[256,2048]{1,0:T(8,128)(2,1)} %get-tuple-element.20), channel_id=1, source_target_pairs={{2,0},{4,2},{6,4},{8,6},{10,8},{12,10},{14,12},{16,14},{18,16},{20... | collective-permute-start | bytes 3145736 | tf_op jit(solution)/shard_map/ppermute | solution.py:152
  186.5 41.3 %collective-permute-start.17 = (bf16[1024,2048]{1,0:T(8,128)(2,1)}, bf16[1024,2048]{1,0:T(8,128)(2,1)}, u32[]{:S(2)}, u32[]{:S(2)}) collective-permute-start(bf16[1024,2048]{1,0:T(8,128)(2,1)} %convolution_convert_fusion), channel_id=1, source_target_pairs={{0,2},{2,0},{4,6},{6,4},{8,10},{10,8},{12,14},{14,12},{16,18},{18,... | collective-permute-start | bytes 12582920 | tf_op jit(solution)/shard_map/ppermute | solution.py:127
  186.5 6.4 %slice-start = ((s8[8388608]{0:T(1024)(128)(4,1)}), s8[4194304]{0:T(1024)(128)(4,1)S(1)}, s32[]{:S(2)}) async-start(s8[8388608]{0:T(1024)(128)(4,1)} %bitcast.107), calls=%async_computation | async-start | bytes 8388608
  189.3 4.2 slice-start.1
  193.5 6.3 %copy-start.13 = (bf16[1024,8,1,128]{0,3,1,2:T(8,128)(2,1)S(1)}, bf16[1024,8,1,128]{0,3,1,2:T(8,128)(2,1)}, u32[]{:S(2)}) copy-start(bf16[1024,8,1,128]{0,3,1,2:T(8,128)(2,1)} %copy.35) | copy-start | bytes 6291460
  199.8 6.2 %copy-start.9 = (bf16[1024,2048]{1,0:T(8,128)(2,1)}, bf16[1024,2048]{1,0:T(8,128)(2,1)S(1)}, u32[]{:S(2)}) copy-start(bf16[1024,2048]{1,0:T(8,128)(2,1)S(1)} %get-tuple-element.11) | copy-start | bytes 12582916
  206.0 33.0 %collective-permute-start.8 = (bf16[1024,2048]{1,0:T(8,128)(2,1)}, bf16[1024,2048]{1,0:T(8,128)(2,1)}, u32[]{:S(2)}, u32[]{:S(2)}) collective-permute-start(bf16[1024,2048]{1,0:T(8,128)(2,1)} %convolution_convert_fusion.1), channel_id=1, source_target_pairs={{0,2},{2,0},{4,6},{6,4},{8,10},{10,8},{12,14},{14,12},{16,18},{18,... | collective-permute-start | bytes 12582920 | tf_op jit(solution)/shard_map/ppermute | solution.py:127
  227.8 12.7 %copy-start.10 = (bf16[1024,2048]{1,0:T(8,128)(2,1)S(1)}, bf16[1024,2048]{1,0:T(8,128)(2,1)}, u32[]{:S(2)}) copy-start(bf16[1024,2048]{1,0:T(8,128)(2,1)} %copy-done.9) | copy-start | bytes 12582916
  227.8 12.7 %copy-start.14 = (bf16[1024,8,1,128]{0,3,1,2:T(8,128)(2,1)S(1)}, bf16[1024,8,1,128]{0,3,1,2:T(8,128)(2,1)}, u32[]{:S(2)}) copy-start(bf16[1024,8,1,128]{0,3,1,2:T(8,128)(2,1)} %copy.34) | copy-start | bytes 6291460
  236.5 3.9 copy-start.7
  238.5 48.8 %collective-permute-start.18 = (bf16[4,2,1,64,2048]{4,3,1,2,0:T(8,128)(2,1)}, bf16[4,2,1,64,2048]{4,3,1,2,0:T(8,128)(2,1)}, u32[]{:S(2)}, u32[]{:S(2)}) collective-permute-start(bf16[4,2,1,64,2048]{4,3,1,2,0:T(8,128)(2,1)} %bitcast_convert_fusion), channel_id=1, source_target_pairs={{0,1},{1,0},{2,3},{3,2},{4,5},{5,4},{6,7},{7,6},{8,9},{9,8},{10,11... | collective-permute-start | bytes 6291464 | tf_op jit(solution)/shard_map/ppermute | solution.py:88
  246.8 3.2 copy-start.5
  251.6 79.6 %collective-permute-start.9 = (bf16[4,2,1,64,2048]{4,3,1,2,0:T(8,128)(2,1)}, bf16[4,2,1,64,2048]{4,3,1,2,0:T(8,128)(2,1)}, u32[]{:S(2)}, u32[]{:S(2)}) collective-permute-start(bf16[4,2,1,64,2048]{4,3,1,2,0:T(8,128)(2,1)} %bitcast_convert_fusion.1), channel_id=1, source_target_pairs={{0,1},{1,0},{2,3},{3,2},{4,5},{5,4},{6,7},{7,6},{8,9},{9,8},{10,11... | collective-permute-start | bytes 6291464 | tf_op jit(solution)/shard_map/ppermute | solution.py:88
  275.2 17.3 %copy-start.12 = (bf16[1536,2048]{1,0:T(8,128)(2,1)S(1)}, bf16[1536,2048]{1,0:T(8,128)(2,1)}, u32[]{:S(2)}) copy-start(bf16[1536,2048]{1,0:T(8,128)(2,1)} %get-tuple-element.41) | copy-start | bytes 18874372
  290.7 43.1 %copy-start.1 = (f32[4,2,1,64,2048]{4,3,1,2,0:T(8,128)}, f32[4,2,1,64,2048]{4,3,1,2,0:T(8,128)S(1)}, u32[]{:S(2)}) copy-start(f32[4,2,1,64,2048]{4,3,1,2,0:T(8,128)S(1)} %bitcast_add_fusion) | copy-start | bytes 12582916
  290.7 40.6 %copy-start.6 = (f32[1024,2048]{1,0:T(8,128)S(1)}, f32[1024,2048]{1,0:T(8,128)}, u32[]{:S(2)}) copy-start(f32[1024,2048]{1,0:T(8,128)} %copy-done.5) | copy-start | bytes 25165828
  291.7 5.9 %collective-permute-start.19 = (bf16[2,64,2048]{2,1,0:T(8,128)(2,1)S(1)}, bf16[2,64,2048]{2,1,0:T(8,128)(2,1)S(1)}, u32[]{:S(2)}, u32[]{:S(2)}) collective-permute-start(bf16[2,64,2048]{2,1,0:T(8,128)(2,1)S(1)} %get-tuple-element.23), channel_id=1, source_target_pairs={{0,8},{2,10},{4,12},{6,14},{1,9},{3,11},{5,13},{7,15}} | collective-permute-start | bytes 1572872 | tf_op jit(solution)/shard_map/ppermute | solution.py:103
  293.7 99.0 %collective-permute-start.6 = (bf16[256,2048]{1,0:T(8,128)(2,1)}, bf16[256,2048]{1,0:T(8,128)(2,1)}, u32[]{:S(2)}, u32[]{:S(2)}) collective-permute-start(bf16[256,2048]{1,0:T(8,128)(2,1)} %get-tuple-element.17), channel_id=1, source_target_pairs={{0,2},{2,4},{4,6},{6,8},{8,10},{10,12},{12,14},{14,16},{16,18},{18... | collective-permute-start | bytes 3145736 | tf_op jit(solution)/shard_map/ppermute | solution.py:155
  293.7 99.0 %collective-permute-start.7 = (bf16[256,2048]{1,0:T(8,128)(2,1)S(1)}, bf16[256,2048]{1,0:T(8,128)(2,1)}, u32[]{:S(2)}, u32[]{:S(2)}) collective-permute-start(bf16[256,2048]{1,0:T(8,128)(2,1)S(1)} %get-tuple-element.18), channel_id=1, source_target_pairs={{2,0},{4,2},{6,4},{8,6},{10,8},{12,10},{14,12},{16,14},{18,16},{20... | collective-permute-start | bytes 3145736 | tf_op jit(solution)/shard_map/ppermute | solution.py:152
  296.3 86.6 %collective-permute-start.22 = (bf16[2,64,2048]{2,1,0:T(8,128)(2,1)}, bf16[2,64,2048]{2,1,0:T(8,128)(2,1)}, u32[]{:S(2)}, u32[]{:S(2)}) collective-permute-start(bf16[2,64,2048]{2,1,0:T(8,128)(2,1)} %get-tuple-element.24), channel_id=1, source_target_pairs={{24,16},{26,18},{28,20},{30,22},{25,17},{27,19},{29,21},{31,23}} | collective-permute-start | bytes 1572872 | tf_op jit(solution)/shard_map/ppermute | solution.py:104
  298.5 84.3 %collective-permute-start.20 = (bf16[2,64,2048]{2,1,0:T(8,128)(2,1)}, bf16[2,64,2048]{2,1,0:T(8,128)(2,1)}, u32[]{:S(2)}, u32[]{:S(2)}) collective-permute-start(bf16[2,64,2048]{2,1,0:T(8,128)(2,1)} %fusion.48), channel_id=1, source_target_pairs={{0,8},{2,10},{4,12},{6,14},{8,16},{10,18},{12,20},{14,22},{1,9},{3... | collective-permute-start | bytes 1572872 | tf_op jit(solution)/shard_map/ppermute | solution.py:103
  333.8 2.3 copy-start.3
  336.1 53.7 %collective-permute-start.10 = (bf16[2,64,2048]{2,1,0:T(8,128)(2,1)}, bf16[2,64,2048]{2,1,0:T(8,128)(2,1)}, u32[]{:S(2)}, u32[]{:S(2)}) collective-permute-start(bf16[2,64,2048]{2,1,0:T(8,128)(2,1)} %get-tuple-element.29), channel_id=1, source_target_pairs={{0,8},{2,10},{4,12},{6,14},{1,9},{3,11},{5,13},{7,15}} | collective-permute-start | bytes 1572872 | tf_op jit(solution)/shard_map/ppermute | solution.py:103
  385.0 26.5 %copy-start.4 = (f32[4,2,1,64,2048]{4,3,1,2,0:T(8,128)S(1)}, f32[4,2,1,64,2048]{4,3,1,2,0:T(8,128)}, u32[]{:S(2)}) copy-start(f32[4,2,1,64,2048]{4,3,1,2,0:T(8,128)} %copy-done.3) | copy-start | bytes 12582916
  385.0 28.8 %collective-permute-start.23 = (bf16[2,64,2048]{2,1,0:T(8,128)(2,1)S(1)}, bf16[2,64,2048]{2,1,0:T(8,128)(2,1)S(1)}, u32[]{:S(2)}, u32[]{:S(2)}) collective-permute-start(bf16[2,64,2048]{2,1,0:T(8,128)(2,1)S(1)} %get-tuple-element.22), channel_id=1, source_target_pairs={{16,8},{18,10},{20,12},{22,14},{24,16},{26,18},{28,20},{30,22},{17... | collective-permute-start | bytes 1572872 | tf_op jit(solution)/shard_map/ppermute | solution.py:104
  388.6 23.0 %collective-permute-start.13 = (bf16[2,64,2048]{2,1,0:T(8,128)(2,1)}, bf16[2,64,2048]{2,1,0:T(8,128)(2,1)S(1)}, u32[]{:S(2)}, u32[]{:S(2)}) collective-permute-start(bf16[2,64,2048]{2,1,0:T(8,128)(2,1)} %get-tuple-element.30), channel_id=1, source_target_pairs={{24,16},{26,18},{28,20},{30,22},{25,17},{27,19},{29,21},{31,23}} | collective-permute-start | bytes 1572872 | tf_op jit(solution)/shard_map/ppermute | solution.py:104
  391.4 20.2 %collective-permute-start.11 = (bf16[2,64,2048]{2,1,0:T(8,128)(2,1)S(1)}, bf16[2,64,2048]{2,1,0:T(8,128)(2,1)S(1)}, u32[]{:S(2)}, u32[]{:S(2)}) collective-permute-start(bf16[2,64,2048]{2,1,0:T(8,128)(2,1)S(1)} %fusion.53), channel_id=1, source_target_pairs={{0,8},{2,10},{4,12},{6,14},{8,16},{10,18},{12,20},{14,22},{1,9},{3... | collective-permute-start | bytes 1572872 | tf_op jit(solution)/shard_map/ppermute | solution.py:103
  392.7 21.1 %copy-start.2 = (f32[4,2,1,64,2048]{4,3,1,2,0:T(8,128)S(1)}, f32[4,2,1,64,2048]{4,3,1,2,0:T(8,128)}, u32[]{:S(2)}) copy-start(f32[4,2,1,64,2048]{4,3,1,2,0:T(8,128)} %copy-done.1) | copy-start | bytes 12582916
  396.4 34.3 %collective-permute-start.21 = (bf16[2,64,2048]{2,1,0:T(8,128)(2,1)S(1)}, bf16[2,64,2048]{2,1,0:T(8,128)(2,1)S(1)}, u32[]{:S(2)}, u32[]{:S(2)}) collective-permute-start(bf16[2,64,2048]{2,1,0:T(8,128)(2,1)S(1)} %get-tuple-element.21), channel_id=1, source_target_pairs={{0,8},{2,10},{4,12},{6,14},{8,16},{10,18},{12,20},{14,22},{16,24},... | collective-permute-start | bytes 1572872 | tf_op jit(solution)/shard_map/ppermute | solution.py:103
  411.8 16.8 %collective-permute-start.14 = (bf16[2,64,2048]{2,1,0:T(8,128)(2,1)S(1)}, bf16[2,64,2048]{2,1,0:T(8,128)(2,1)S(1)}, u32[]{:S(2)}, u32[]{:S(2)}) collective-permute-start(bf16[2,64,2048]{2,1,0:T(8,128)(2,1)S(1)} %get-tuple-element.28), channel_id=1, source_target_pairs={{16,8},{18,10},{20,12},{22,14},{24,16},{26,18},{28,20},{30,22},{17... | collective-permute-start | bytes 1572872 | tf_op jit(solution)/shard_map/ppermute | solution.py:104
  413.9 25.9 %collective-permute-start.24 = (bf16[2,64,2048]{2,1,0:T(8,128)(2,1)S(1)}, bf16[2,64,2048]{2,1,0:T(8,128)(2,1)S(1)}, u32[]{:S(2)}, u32[]{:S(2)}) collective-permute-start(bf16[2,64,2048]{2,1,0:T(8,128)(2,1)S(1)} %fusion.47), channel_id=1, source_target_pairs={{8,0},{10,2},{12,4},{14,6},{16,8},{18,10},{20,12},{22,14},{24,16},... | collective-permute-start | bytes 1572872 | tf_op jit(solution)/shard_map/ppermute | solution.py:104
  418.1 22.3 %collective-permute-start.12 = (bf16[2,64,2048]{2,1,0:T(8,128)(2,1)S(1)}, bf16[2,64,2048]{2,1,0:T(8,128)(2,1)S(1)}, u32[]{:S(2)}, u32[]{:S(2)}) collective-permute-start(bf16[2,64,2048]{2,1,0:T(8,128)(2,1)S(1)} %get-tuple-element.27), channel_id=1, source_target_pairs={{0,8},{2,10},{4,12},{6,14},{8,16},{10,18},{12,20},{14,22},{16,24},... | collective-permute-start | bytes 1572872 | tf_op jit(solution)/shard_map/ppermute | solution.py:103
  428.7 19.7 %collective-permute-start.15 = (bf16[2,64,2048]{2,1,0:T(8,128)(2,1)S(1)}, bf16[2,64,2048]{2,1,0:T(8,128)(2,1)S(1)}, u32[]{:S(2)}, u32[]{:S(2)}) collective-permute-start(bf16[2,64,2048]{2,1,0:T(8,128)(2,1)S(1)} %fusion.52), channel_id=1, source_target_pairs={{8,0},{10,2},{12,4},{14,6},{16,8},{18,10},{20,12},{22,14},{24,16},... | collective-permute-start | bytes 1572872 | tf_op jit(solution)/shard_map/ppermute | solution.py:104
  440.1 8.7 %collective-permute-start.25 = (bf16[1,64,2048]{2,1,0:T(8,128)(2,1)S(1)}, bf16[1,64,2048]{2,1,0:T(8,128)(2,1)S(1)}, u32[]{:S(2)}, u32[]{:S(2)}) collective-permute-start(bf16[1,64,2048]{2,1,0:T(8,128)(2,1)S(1)} %dynamic-slice_convert_fusion.4), channel_id=1, source_target_pairs={{0,4},{2,6},{4,0},{6,2},{8,12},{10,14},{12,8},{14,10},{16,20},{18,... | collective-permute-start | bytes 786440 | tf_op jit(solution)/shard_map/ppermute | solution.py:88
  448.6 6.4 %collective-permute-start.16 = (bf16[1,64,2048]{2,1,0:T(8,128)(2,1)S(1)}, bf16[1,64,2048]{2,1,0:T(8,128)(2,1)S(1)}, u32[]{:S(2)}, u32[]{:S(2)}) collective-permute-start(bf16[1,64,2048]{2,1,0:T(8,128)(2,1)S(1)} %dynamic-slice_convert_fusion.5), channel_id=1, source_target_pairs={{0,4},{2,6},{4,0},{6,2},{8,12},{10,14},{12,8},{14,10},{16,20},{18,... | collective-permute-start | bytes 786440 | tf_op jit(solution)/shard_map/ppermute | solution.py:88

commit v2 on v0

v2 whole, which is shorter than its diff:
```python
import jax
import jax.numpy as jnp
from jax import lax
from jax.experimental import pallas as pl
from jax.experimental.pallas import tpu as pltpu
from jax.sharding import PartitionSpec as P

BAND = 256
BF = jnp.bfloat16
F32 = jnp.float32
LANES = 128
STEP = 512
PARTS = 2
VMEM = 56 << 20
SCALE = 0.7978845608
CUBIC = 0.044715


def dot(a, b, contract=((1,), (0,))):
    return lax.dot_general(a, b, (contract, ((), ())), preferred_element_type=F32)


def sds(shape, dtype):
    return jax.ShapeDtypeStruct(shape, dtype)


def call(body, steps, in_specs, out_specs, out_shape, flops, scratch=(), prefetch=0, after=()):
    inputs = prefetch + len(in_specs)
    in_specs = list(in_specs) + [pl.BlockSpec(memory_space=pl.ANY)] * len(after)

    def kernel(*refs):
        body(*refs[:inputs], *refs[inputs + len(after) :])

    made = pl.pallas_call(
        kernel,
        grid_spec=pltpu.PrefetchScalarGridSpec(
            num_scalar_prefetch=prefetch,
            grid=(steps,),
            in_specs=in_specs,
            out_specs=out_specs,
            scratch_shapes=scratch,
        ),
        out_shape=out_shape,
        compiler_params=pltpu.CompilerParams(vmem_limit_bytes=VMEM),
        cost_estimate=pl.CostEstimate(flops=flops, bytes_accessed=1 << 12, transcendentals=0),
    )
    return lambda *args: made(*args, *after)


def full(shape):
    return pl.BlockSpec(shape, lambda j, *_: (0,) * len(shape))


def cols(rows, base=0, count=None, width=STEP, start=0):
    if count is None:
        return pl.BlockSpec((rows, width), lambda j, *_: (0, start + j))
    return pl.BlockSpec((rows, width), lambda j, *_: (0, jnp.clip(j - base, 0, count - 1)))


def rows_of(width, base, count, height=STEP):
    return pl.BlockSpec((height, width), lambda j, *_: (jnp.clip(j - base, 0, count - 1), 0))


def count_own(core, slots, degree, field):
    nodes, slot_total = slots.shape
    width = field.shape[1]
    quarter = (nodes + 2 * BAND) // 4
    groups, steps = nodes // LANES, width // STEP
    pieces = LANES // 8

    def count(core_ref, slots_ref, degree_ref, t_own, t_halo, n_own, n_halo, key_ref, value_ref):
        group = pl.program_id(0)
        slot = slots_ref[...]
        q = (
            (slot >= quarter).astype(jnp.int32)
            + (slot >= 2 * quarter).astype(jnp.int32)
            + (slot >= 3 * quarter).astype(jnp.int32)
        )
        used = lax.broadcasted_iota(jnp.int32, slot.shape, 0) < degree_ref[...]
        key_ref[...] = slot - q * quarter
        value_ref[...] = jnp.where(used, jnp.left_shift(1, q * 8), 0)
        sub = lax.broadcasted_iota(jnp.int32, (8, LANES), 0)
        row = lax.broadcasted_iota(jnp.int32, (LANES, LANES), 0)
        col = lax.broadcasted_iota(jnp.int32, (LANES, LANES), 1)
        nodes_at = pl.ds(pl.multiple_of(group * LANES, LANES), LANES)
        for part in range(quarter // LANES):

            def add_slot(k, packed):
                key = jnp.broadcast_to(key_ref[pl.ds(k, 1), :], (8, LANES)) - sub
                value = jnp.broadcast_to(value_ref[pl.ds(k, 1), :], (8, LANES))
                return tuple(
                    acc + jnp.where(key == part * LANES + 8 * i, value, 0)
                    for i, acc in enumerate(packed)
                )

            packed = lax.fori_loop(
                0,
                slot_total,
                add_slot,
                tuple(jnp.zeros((8, LANES), jnp.int32) for _ in range(pieces)),
                unroll=4,
            )
            packed = jnp.concatenate(packed, axis=0)
            for q in range(4):
                counts = jnp.bitwise_and(jnp.right_shift(packed, 8 * q), 255)
                start = q * quarter + part * LANES
                own = start - BAND
                if 0 <= own < nodes:
                    counts = counts + jnp.where(row + own == col + group * LANES, 2, 0)
                    counts = counts.astype(F32)
                    t_own[own : own + LANES, :] = counts.astype(BF)
                    n_own[nodes_at, own : own + LANES] = counts.T.astype(BF)
                else:
                    after = own >= 0
                    inner = start - nodes - BAND if after else start
                    slot_of = core_ref[0] if after else 1 - core_ref[0]
                    at = pl.ds(pl.multiple_of(slot_of * BAND + inner, LANES), LANES)
                    counts = counts.astype(F32)
                    t_halo[at, :] = counts.astype(BF)
                    n_halo[nodes_at, at] = counts.T.astype(BF)

    def body(core_ref, slots_ref, degree_ref, f_ref, t_own, t_halo, n_own, n_halo, out, *scratch):
        step = pl.program_id(0)

        @pl.when(step < groups)
        def _():
            count(core_ref, slots_ref, degree_ref, t_own, t_halo, n_own, n_halo, *scratch)

        @pl.when(step >= groups)
        def _():
            out[...] = dot(n_own[...], f_ref[...]).astype(BF)

    tall = lambda h: cols(h, 0, groups, LANES)
    return call(
        body,
        groups + steps,
        [tall(slot_total), tall(1), cols(nodes, groups, steps)],
        [
            tall(nodes),
            tall(2 * BAND),
            full((nodes, nodes)),
            full((nodes, 2 * BAND)),
            cols(nodes, groups, steps),
        ],
        [
            sds((nodes, nodes), BF),
            sds((2 * BAND, nodes), BF),
            sds((nodes, nodes), BF),
            sds((nodes, 2 * BAND), BF),
            sds((nodes, width), BF),
        ],
        flops=20 << 30,
        scratch=[pltpu.VMEM((slot_total, LANES), jnp.int32)] * 2,
        prefetch=1,
    )(core, slots.T, degree[None, :], field)


def own_sum(n_own, field):
    def body(n_ref, f_ref, out):
        out[...] = dot(n_ref[...], f_ref[...]).astype(BF)

    nodes, width = field.shape
    return call(
        body,
        width // STEP,
        [full((nodes, nodes)), cols(nodes)],
        cols(nodes),
        sds((nodes, width), BF),
        flops=2 * nodes * nodes * width,
    )(n_own, field)


def gelu_parts(p):
    square = p * p
    t = jnp.tanh(p * (SCALE + SCALE * CUBIC * square))
    half = 0.5 + 0.5 * t
    slope = half + (0.5 * p) * (1.0 - t * t) * (SCALE + 3.0 * SCALE * CUBIC * square)
    return p * half, slope


def average_step(own_ref, n_ref, near_ref, far_ref, inv_ref, out_t, averaged_ref, step):
    total = own_ref[...].astype(F32) + dot(n_ref[:, :BAND], near_ref[...])
    total = (total + dot(n_ref[:, BAND:], far_ref[...])) * inv_ref[...]
    averaged_ref[step] = total.astype(BF)
    out_t[...] = total.T.astype(BF)


def average_specs(nodes, steps):
    return [
        cols(nodes, 0, steps),
        full((nodes, 2 * BAND)),
        cols(BAND, 0, steps),
        cols(BAND, 0, steps),
        full((nodes, 1)),
    ]


def blocks_dot(blocks_ref, other, across=False):
    total = None
    for k in range(blocks_ref.shape[0]):
        if across:
            part = dot(blocks_ref[k], other[:, k * STEP : (k + 1) * STEP], ((1,), (1,)))
        else:
            part = dot(blocks_ref[k], other[k * STEP : (k + 1) * STEP, :])
        total = part if total is None else total + part
    return total


def first_layer(own, n_halo, near, far, inverse, weight, bias):
    nodes, width = own.shape
    steps = width // STEP

    def body(own_ref, n_ref, near_ref, far_ref, inv_ref, w_ref, b_ref, out_t, hidden, slope, avg):
        step = pl.program_id(0)

        @pl.when(step < steps)
        def _():
            average_step(own_ref, n_ref, near_ref, far_ref, inv_ref, out_t, avg, step)

        @pl.when(step >= steps)
        def _():
            value, grad = gelu_parts(blocks_dot(avg, w_ref) + b_ref[...])
            hidden[...] = value.astype(BF)
            slope[...] = grad.astype(BF)

    return call(
        body,
        2 * steps,
        average_specs(nodes, steps) + [cols(width, steps, steps), cols(1, steps, steps)],
        [rows_of(nodes, 0, steps), cols(nodes, steps, steps), cols(nodes, steps, steps)],
        [sds((width, nodes), BF), sds((nodes, width), BF), sds((nodes, width), BF)],
        flops=2 * nodes * width * (2 * BAND + width),
        scratch=[pltpu.VMEM((steps, nodes, STEP), BF)],
    )(own, n_halo, near, far, inverse, weight, bias)


def second_layer(own, n_halo, near, far, inverse, weight, bias, cotangent, t_halo):
    nodes, width = own.shape
    steps = width // STEP

    def body(
        own_ref, n_ref, near_ref, far_ref, inv_ref, w_ref, b_ref, c_ref, wt_ref, t_ref,
        out_t, activations, grad_pre, scaled, ends, avg, grads,
    ):
        step = pl.program_id(0)

        @pl.when(step < steps)
        def _():
            average_step(own_ref, n_ref, near_ref, far_ref, inv_ref, out_t, avg, step)

        @pl.when((step >= steps) & (step < 2 * steps))
        def _():
            value, grad = gelu_parts(blocks_dot(avg, w_ref) + b_ref[...])
            activations[...] = value.astype(BF)
            grad = (c_ref[...].astype(F32) * grad).astype(BF)
            grad_pre[...] = grad
            grads[step - steps] = grad

        @pl.when(step >= 2 * steps)
        def _():
            back_step(blocks_dot(grads, wt_ref, True), inv_ref, t_ref, scaled, ends)

    return call(
        body,
        3 * steps,
        average_specs(nodes, steps)
        + [
            cols(width, steps, steps),
            cols(1, steps, steps),
            cols(nodes, steps, steps),
            rows_of(width, 2 * steps, steps),
            full((2 * BAND, nodes)),
        ],
        [
            rows_of(nodes, 0, steps),
            cols(nodes, steps, steps),
            cols(nodes, steps, steps),
            cols(nodes, 2 * steps, steps),
            cols(2 * BAND, 2 * steps, steps),
        ],
        [
            sds((width, nodes), BF),
            sds((nodes, width), BF),
            sds((nodes, width), BF),
            sds((nodes, width), BF),
            sds((2 * BAND, width), BF),
        ],
        flops=2 * nodes * width * (4 * BAND + 2 * width),
        scratch=[pltpu.VMEM((steps, nodes, STEP), BF)] * 2,
    )(own, n_halo, near, far, inverse, weight, bias, cotangent, weight, t_halo)


def back_step(grad_averaged, inv_ref, t_ref, scaled_ref, ends_ref):
    scaled = (grad_averaged * inv_ref[...]).astype(BF)
    scaled_ref[...] = scaled
    ends_ref[...] = dot(t_ref[...], scaled).astype(BF)


def back_product(grad_pre, weight, inverse, t_halo, after=()):
    nodes, width = grad_pre[0].shape[0], weight.shape[1]
    steps = width // STEP

    def body(*refs):
        g_refs, (w_ref, inv_ref, t_ref, scaled, ends, token) = refs[:PARTS], refs[PARTS:]
        token[0] = 0
        total, at = 0.0, 0
        for g_ref in g_refs:
            size = g_ref.shape[1]
            total = total + dot(g_ref[...], w_ref[:, at : at + size], ((1,), (1,)))
            at += size
        back_step(total, inv_ref, t_ref, scaled, ends)

    return call(
        body,
        steps,
        [full(g.shape) for g in grad_pre]
        + [
            rows_of(width, 0, steps),
            full((nodes, 1)),
            full((2 * BAND, nodes)),
        ],
        [cols(nodes), cols(2 * BAND), pl.BlockSpec(memory_space=pltpu.SMEM)],
        [sds((nodes, width), BF), sds((2 * BAND, width), BF), sds((1,), jnp.int32)],
        flops=2 * nodes * width * (width + 2 * BAND),
        after=after,
    )(*grad_pre, weight, inverse, t_halo)


def back_sum_step(core_ref, s_ref, t_ref, near_ref, far_ref, slope_ref):
    nodes = t_ref.shape[0]
    total = dot(t_ref[...], s_ref[...])
    near, far = near_ref[...].astype(F32), far_ref[...].astype(F32)
    odd = core_ref[0] == 1
    pieces = (
        (0, BAND, total[:BAND] + jnp.where(odd, near, far)),
        (BAND, nodes - BAND, total[BAND : nodes - BAND]),
        (nodes - BAND, nodes, total[nodes - BAND :] + jnp.where(odd, far, near)),
    )
    for lo, hi, value in pieces:
        if slope_ref is not None:
            value = value * slope_ref[lo:hi, :].astype(F32)
        yield lo, hi, value.astype(BF)


def back_sum(core, scaled, t_own, near, far, after=()):
    def body(core_ref, s_ref, t_ref, near_ref, far_ref, out, token):
        token[0] = 0
        for lo, hi, value in back_sum_step(core_ref, s_ref, t_ref, near_ref, far_ref, None):
            out[lo:hi, :] = value

    nodes, width = scaled.shape
    return call(
        body,
        width // STEP,
        [cols(nodes), full((nodes, nodes)), cols(BAND), cols(BAND)],
        [cols(nodes), pl.BlockSpec(memory_space=pltpu.SMEM)],
        [sds((nodes, width), BF), sds((1,), jnp.int32)],
        flops=2 * nodes * nodes * width,
        prefetch=1,
        after=after,
    )(core, scaled, t_own, near, far)


def half_view(averaged_t):
    width, nodes = averaged_t.shape
    blk = lax.axis_size("blk")
    return averaged_t.reshape(blk // 2, 2, width // blk, nodes)


def half_spec(view, flip):
    pairs, _, run, nodes = view.shape
    pick = lambda j, core: (0, 1 - core[0] if flip else core[0], 0, 0)
    return pl.BlockSpec((pairs, 1, run, nodes), pick)


def half_dot(a_ref, g):
    pairs, _, run, nodes = a_ref.shape
    return dot(a_ref[...].reshape(pairs * run, nodes), g).astype(BF)


def weight_half(core, averaged_t, grad_pre, flip, after=()):
    width = sum(g.shape[1] for g in grad_pre)
    nodes = grad_pre[0].shape[0]
    view = half_view(averaged_t)
    half = view.shape[0] * view.shape[2]
    each = width // PARTS // STEP

    def part_cols(rows, part):
        return cols(rows, part * each, each)

    def body(core_ref, a_ref, *refs):
        g_refs, outs, bias = refs[: len(grad_pre)], refs[len(grad_pre) :][:PARTS], refs[-1]
        for part in range(PARTS):

            @pl.when(pl.program_id(0) // each == part)
            def _():
                g_ref = g_refs[part % len(g_refs)]
                outs[part][...] = half_dot(a_ref, g_ref[...])
                if flip:
                    bias[...] = jnp.sum(g_ref[...].astype(F32), axis=0, keepdims=True)

    if len(grad_pre) == 1:
        g_specs = [cols(nodes)]
    else:
        g_specs = [part_cols(nodes, part) for part in range(PARTS)]
    return call(
        body,
        width // STEP,
        [half_spec(view, flip)] + g_specs,
        [part_cols(half, part) for part in range(PARTS)] + [cols(1)] * flip,
        [sds((half, width // PARTS), BF)] * PARTS + [sds((1, width), F32)] * flip,
        flops=(2 if flip else 16) * nodes * half * width,
        prefetch=1,
        after=after,
    )(core, view, *grad_pre)


def back_sum_weight(core, scaled, t_own, near, far, slope, averaged_t, part, after=()):
    nodes, width = scaled.shape
    view = half_view(averaged_t)
    half = view.shape[0] * view.shape[2]
    width //= PARTS
    start = part * width // STEP

    def body(core_ref, s_ref, t_ref, near_ref, far_ref, p_ref, a_ref, grad_pre, send, bias):
        for lo, hi, value in back_sum_step(core_ref, s_ref, t_ref, near_ref, far_ref, p_ref):
            grad_pre[lo:hi, :] = value
        grad = grad_pre[...]
        bias[...] = jnp.sum(grad.astype(F32), axis=0, keepdims=True)
        send[...] = half_dot(a_ref, grad)

    return call(
        body,
        width // STEP,
        [
            cols(nodes, start=start),
            full((nodes, nodes)),
            cols(BAND, start=start),
            cols(BAND, start=start),
            cols(nodes, start=start),
            half_spec(view, True),
        ],
        [cols(nodes), cols(half), cols(1)],
        [sds((nodes, width), BF), sds((half, width), BF), sds((1, width), F32)],
        flops=2 * nodes * width * (nodes + half),
        prefetch=1,
        after=after,
    )(core, scaled, t_own, near, far, slope, view)


def swap(axis, distance):
    return [(i, i ^ distance) for i in range(lax.axis_size(axis))]


def exchange(near, far):
    count = lax.axis_size("blk")
    other = [(i, (i + 1 if i % 2 else i - 1) % count) for i in range(count)]
    return lax.ppermute(near, "blk", swap("blk", 1)), lax.ppermute(far, "blk", other)


def field_halo(field):
    nodes = field.shape[0]
    odd = lax.axis_index("blk") % 2
    rows = lambda last: lax.dynamic_slice_in_dim(field, last * (nodes - BAND), BAND, 0)
    return exchange(rows(1 - odd), rows(odd))


def place_bits():
    b, g = lax.axis_index("blk"), lax.axis_index("grp")
    line = (lax.axis_size("blk") // 4).bit_length() - 1
    across = lax.axis_size("grp").bit_length() - 1
    bits = [(b // (4 << i)) % 2 for i in reversed(range(line))] + [(b // 2) % 2]
    return bits + [(g // (1 << i)) % 2 for i in reversed(range(across))]


def steps_of(axis):
    line = (lax.axis_size("blk") // 4).bit_length() - 1
    across = lax.axis_size("grp").bit_length() - 1
    if axis == "y":
        return [(line, "blk", 2)]
    if axis == "x":
        return [(line + 1 + i, "grp", 1 << (across - 1 - i)) for i in range(across)]
    return [(line - 1 - axis, "blk", 4 << axis)] if axis < line else []


class PartSum:
    def __init__(self, terms, order):
        self.bits = place_bits()
        self.terms = [t.reshape((2,) * len(self.bits) + (-1, t.shape[-1])) for t in terms]
        self.todo = [step for axis in order for step in steps_of(axis)]
        self.settled = []

    def sum(self, flip=None, token=0):
        total = 0.0
        for term in self.terms:
            at, sizes = [], []
            for dim, bit in enumerate(self.bits):
                pick = term.shape[dim] == 2 and dim in self.settled
                at.append((1 - bit if dim == flip else bit) + token if pick else 0)
                sizes.append(1 if pick else term.shape[dim])
            total = total + lax.dynamic_slice(
                term, (*at, 0, 0), (*sizes, *term.shape[-2:])
            ).astype(F32)
        return total

    def step(self, token=0):
        dim, axis, distance = self.todo.pop(0)
        self.settled.append(dim)
        sent = self.sum(dim, token).astype(self.terms[0].dtype)
        self.terms = self.terms + [lax.ppermute(sent, axis, swap(axis, distance))]
        return sent

    def result(self):
        while self.todo:
            self.step()
        return self.sum().reshape(self.terms[0].shape[-2:])


def orders(kind):
    rest = range(1, (lax.axis_size("blk") // 4).bit_length() - 1)
    return {
        "xyz": ["x", "y", 0, *rest],
        "yxz": ["y", "x", 0, *rest],
        "xzy": ["x", 0, *rest, "y"],
        "zxy": [0, "x", *rest, "y"],
        "xzyz": ["x", 0, "y", *rest],
        "zxyz": [0, "x", "y", *rest],
    }[kind]


class WeightSum:
    def __init__(self, send, keep, kinds):
        self.parts = [
            PartSum([mine, lax.ppermute(theirs, "blk", swap("blk", 1))], orders(kind))
            for mine, theirs, kind in zip(keep, send, kinds)
        ]

    def step(self, token=0):
        return [part.step(token) for part in self.parts]

    def result(self):
        return jnp.concatenate([part.result() for part in self.parts], axis=1)


def bias_sum(biases, token):
    blk, grp = lax.axis_size("blk"), lax.axis_size("grp")
    bit = lax.axis_index("blk") % 2
    count = biases.shape[0]
    by_core = biases.reshape(count, blk // 2, 2, grp, -1).transpose(2, 1, 3, 0, 4)
    half = lambda which: lax.dynamic_index_in_dim(by_core, which + token, 0, keepdims=False)
    total = half(bit) + lax.ppermute(half(1 - bit), "blk", swap("blk", 1))
    return PartSum([total.reshape(blk // 2 * grp * count, -1)], orders("xyz")).result()


def local(features, neighbours, degree, weight_one, bias_one, weight_two, bias_two, cotangent):
    core = (lax.axis_index("blk") % 2).reshape(1).astype(jnp.int32)
    inverse = 1.0 / (degree[0].astype(F32)[:, None] + 1.0)
    field = features[0]

    near, far = field_halo(field)
    t_own, t_halo, n_own, n_halo, own = count_own(core, neighbours[0], degree[0], field)
    averaged_one, hidden, slope = first_layer(
        own, n_halo, near, far, inverse, weight_one, bias_one[None, :]
    )
    near, far = field_halo(hidden)
    own = own_sum(n_own, hidden)
    averaged_two, activations, grad_pre_two, scaled, ends = second_layer(
        own, n_halo, near, far, inverse, weight_two, bias_two[None, :], cotangent[0], t_halo
    )
    near, far = exchange(ends[:BAND], ends[BAND:])
    *send, grad_bias_two = weight_half(core, averaged_two, [grad_pre_two], True)
    keep = weight_half(core, averaged_two, [grad_pre_two], False, send)
    sum_two = WeightSum(send, keep, ["xyz", "yxz"])

    grad_pre_one, sends, grad_bias_one, after = [], [], [], sum_two.step()
    for part in range(PARTS):
        grad, send, bias = back_sum_weight(
            core, scaled, t_own, near, far, slope, averaged_one, part, after
        )
        grad_pre_one.append(grad)
        sends.append(send)
        grad_bias_one.append(bias)
        after = [send]
    keep = weight_half(core, averaged_one, grad_pre_one, False, sends)
    sum_one = WeightSum(sends, keep, ["xzyz", "zxyz"])
    sent = sum_one.step()
    scaled, ends, token = back_product(grad_pre_one, weight_one, inverse, t_halo, sent)
    near, far = exchange(ends[:BAND], ends[BAND:])
    sent = sum_two.step(token[0]) + sum_one.step(token[0])
    grad_input, token = back_sum(core, scaled, t_own, near, far, sent)
    sum_one.step(token[0])
    sum_two.step(token[0])
    grad_one, grad_two = sum_one.result(), sum_two.result()
    grad_bias_one = jnp.concatenate(grad_bias_one, axis=1)
    biases = bias_sum(jnp.concatenate([grad_bias_one, grad_bias_two]), token[0])
    return activations[None], grad_input[None], grad_one, biases[0], grad_two, biases[1]


def solution(mesh):
    rows = P("grp", "blk", None)
    spread = ("blk", "grp")
    return jax.shard_map(
        local,
        mesh=mesh,
        in_specs=(rows, rows, P("grp", "blk"), P(), P(), P(), P(), rows),
        out_specs=(rows, rows, P(spread, None), P(spread), P(spread, None), P(spread)),
        check_vma=False,
    )
```

time: 1170 us -> 319 us (0.27)
  waiting for transfers between devices: 561 us -> 44.8 us
  other arithmetic: 311 us -> 35.7 us
  Pallas kernels: 0 us -> 162 us
  matrix products: 116 us -> 0 us
  blocking collectives: 54.3 us -> 0 us
  local copies, waits for them, and re-layouts: 67.3 us -> 15.1 us
  starting transfers between devices: 34 us -> 45.8 us
    reduce_scatter x2 -> x0, waiting for transfers between devices: 539 us -> none  [reduce_grads(): lax.psum_scatter(grad_weight, ('blk', 'grp'), scatter_dimension=0, tiled=...]
    reduce_sum x17 -> x0, other arithmetic: 243 us -> none  [the longest x16 234 us: add_block(): return counts + jnp.sum(match * block_used[:, :, None], axis=1)]
    pallas_call x0 -> x11, Pallas kernels: none -> 162 us  [call(): return lambda *args: made(*args, *after)]
    dot_general x10 -> x0, matrix products: 116 us -> none  [the longest x2 31.2 us: aggregate(): jnp.dot(averaged, weight, preferred_element_type=jnp.float32) + bias_vec]
    unnamed x1 -> x0, blocking collectives: 54.3 us -> none
    add x19 -> x5, other arithmetic: 49.2 us -> 0.05 us  [the longest x4 0.04 us: sum(): total + lax.dynamic_slice(term, (*at, 0, 0), (*sizes, *term.shape[-2:]))....]
    while x64 -> x0, local copies, waits for them, and re-layouts: 42 us -> none
    convert_element_type x2 -> x16, other arithmetic: 4.03 us -> 29.1 us  [step(): sent = self.sum(dim, token).astype(self.terms[0].dtype)]
  transfers between devices with their start and end apart: 10 -> 33, of which waited for: 5 -> 12; matrix products, arithmetic and copies ran while one was open for 33% -> 12% of each run, Pallas kernels for 0% -> 30%
where the time goes in v2:
time: 319 us; the launch traced here: 313 us
  Pallas kernels  162 us (51%)
  starting transfers between devices  45.8 us (14%)
  waiting for transfers between devices  44.8 us (14%)
  other arithmetic  35.7 us (11%)
  local copies, waits for them, and re-layouts  15.1 us (5%)
  between operations  9.53 us (3%)
    pallas_call x11, Pallas kernels, call(): return lambda *args: made(*args, *after)  162 us
    ppermute x20, waiting for transfers between devices, step(): self.terms = self.terms + [lax.ppermute(sent, axis, swap(axis, distance))]  38.9 us
    convert_element_type x16, other arithmetic, step(): sent = self.sum(dim, token).astype(self.terms[0].dtype)  29.1 us
    ppermute x20, starting transfers between devices, step(): self.terms = self.terms + [lax.ppermute(sent, axis, swap(axis, distance))]  21.1 us
    ppermute x4, starting transfers between devices, exchange(): lax.ppermute(near, 'blk', swap('blk', 1))  10.9 us
    ppermute x1, starting transfers between devices, bias_sum(): total = half(bit) + lax.ppermute(half(1 - bit), 'blk', swap('blk', 1))  8.91 us
  transfers between devices with their start and end apart: 33, of which 12 were waited for; matrix products, arithmetic and copies ran while one was open for 12% of the time, Pallas kernels for 30%

profile of v2, /device:TPU:18, one launch (start us, length us, event | category | flops | bytes accessed | tf_op | source)
XLA Modules:
  0.0 313.1 jit_solution(12490785263998662897)
XLA Ops:
  0.7 1.8 dynamic-slice_bitcast_fusion
  2.5 1.5 collective-permute-start.1
  4.1 1.0 copy.16.refs_4_.refs_3_
  5.1 24.8 %shard_map.127 = (bf16[1024,1024]{1,0:T(8,128)(2,1)}, bf16[512,1024]{1,0:T(8,128)(2,1)}, bf16[1024,1024]{1,0:T(8,128)(2,1)}, bf16[1024,512]{1,0:T(8,128)(2,1)}, bf16[1024,2048]{1,0:T(8,128)(2,1)}) custom-call(s32[1]{0:T(128)} %bitcast.refs_0_, s32[64,1024]{1,0:T(8,128)} %bitcast.103, s32[1,1024]{1,0:T(1,128)} %refs_2_.2, bf16[1024,2048]{1,0:T(8,128)(2,1)} %bitcast.96), custom_call_target="tpu_custom_call" | custom-call | flops 21474836480 | bytes 4096 | tf_op jit(solution)/shard_map/pallas_call | solution.py:47
  29.9 1.0 copy-done.16
  30.9 22.5 %shard_map.128 = (bf16[2048,1024]{1,0:T(8,128)(2,1)}, bf16[1024,2048]{1,0:T(8,128)(2,1)}, bf16[1024,2048]{1,0:T(8,128)(2,1)}) custom-call(bf16[1024,2048]{1,0:T(8,128)(2,1)} %get-tuple-element.38.refs_0_, bf16[1024,512]{1,0:T(8,128)(2,1)} %get-tuple-element.39.refs_1_, bf16[256,2048]{1,0:T(8,128)(2,1)} %copy-done.16, ...), custom_call_target="tpu_custom_call" | custom-call | flops 10737418240 | bytes 4096 | tf_op jit(solution)/shard_map/pallas_call | solution.py:47
  53.4 1.8 constant_dynamic-slice_fusion.16
  55.4 1.1 collective-permute-start.3
  56.5 8.4 %shard_map.129.refs_0_ = bf16[1024,2048]{1,0:T(8,128)(2,1)} custom-call(bf16[1024,1024]{1,0:T(8,128)(2,1)} %get-tuple-element.37.refs_0_, bf16[1024,2048]{1,0:T(8,128)(2,1)} %get-tuple-element.40.refs_1_), custom_call_target="tpu_custom_call" | custom-call | flops 4294967296 | bytes 4096 | tf_op jit(solution)/shard_map/pallas_call | solution.py:47
  64.9 5.9 %collective-permute-done.3.refs_3_ = bf16[256,2048]{1,0:T(8,128)(2,1)} collective-permute-done((bf16[256,2048]{1,0:T(8,128)(2,1)S(1)}, bf16[256,2048]{1,0:T(8,128)(2,1)}, u32[]{:S(2)}, u32[]{:S(2)}) %collective-permute-start.3) | collective-permute-done | bytes 1048608 | tf_op jit(solution)/shard_map/ppermute | solution.py:458
  70.8 37.2 %shard_map.130 = (bf16[2048,1024]{1,0:T(8,128)(2,1)}, bf16[1024,2048]{1,0:T(8,128)(2,1)}, bf16[1024,2048]{1,0:T(8,128)(2,1)}, bf16[1024,2048]{1,0:T(8,128)(2,1)}, bf16[512,2048]{1,0:T(8,128)(2,1)}) custom-call(bf16[1024,2048]{1,0:T(8,128)(2,1)} %shard_map.129.refs_0_, bf16[1024,512]{1,0:T(8,128)(2,1)} %get-tuple-element.39.refs_1_, ...), custom_call_target="tpu_custom_call" | custom-call | flops 21474836480 | bytes 4096 | tf_op jit(solution)/shard_map/pallas_call | solution.py:47
  108.0 3.1 fusion.14
  111.1 10.5 %collective-permute-start.4 = (bf16[256,2048]{1,0:T(8,128)(2,1)}, bf16[256,2048]{1,0:T(8,128)(2,1)S(1)}, u32[]{:S(2)}, u32[]{:S(2)}) collective-permute-start(bf16[256,2048]{1,0:T(8,128)(2,1)} %get-tuple-element.75), channel_id=1, source_target_pairs={{0,2},{2,0},{4,6},{6,4},{8,10},{10,8},{12,14},{14,12},{16,18},{18,... | collective-permute-start | bytes 3145736 | tf_op jit(solution)/shard_map/ppermute | solution.py:458
  121.6 1.2 collective-permute-start.5
  122.8 8.7 %shard_map.131 = (bf16[1024,1024]{1,0:T(8,128)(2,1)}, bf16[1024,1024]{1,0:T(8,128)(2,1)}, f32[1,2048]{1,0:T(1,128)}) custom-call(s32[1]{0:T(128)} %bitcast.refs_0_, bf16[8,2,128,1024]{3,2,1,0:T(8,128)(2,1)} %bitcast.108, bf16[1024,2048]{1,0:T(8,128)(2,1)} %get-tuple-element.49.refs_2_), custom_call_target="tpu_custom_call" | custom-call | flops 4294967296 | bytes 4096 | tf_op jit(solution)/shard_map/pallas_call | solution.py:47
  132.0 8.8 %shard_map.132 = (bf16[1024,1024]{1,0:T(8,128)(2,1)}, bf16[1024,1024]{1,0:T(8,128)(2,1)}) custom-call(s32[1]{0:T(128)} %bitcast.refs_0_, bf16[8,2,128,1024]{3,2,1,0:T(8,128)(2,1)} %bitcast.109, bf16[1024,2048]{1,0:T(8,128)(2,1)} %get-tuple-element.49.refs_2_, bf16[1024,1024]{1,0:T(8,128)(2,1)} %get-tuple-element.50.refs_3_, ...), custom_call_target="tpu_custom_call" | custom-call | flops 34359738368 | bytes 4096 | tf_op jit(solution)/shard_map/pallas_call | solution.py:47
  140.8 2.5 add_convert_fusion.3.refs_7_
  143.9 1.4 copy-done.7
  145.3 1.6 add_convert_fusion.2.refs_8_
  147.0 1.6 collective-permute-start.13
  148.6 0.9 copy-done.2
  149.9 9.1 %shard_map.133 = (bf16[1024,1024]{1,0:T(8,128)(2,1)}, bf16[1024,1024]{1,0:T(8,128)(2,1)}, f32[1,1024]{1,0:T(1,128)}) custom-call(s32[1]{0:T(128)} %bitcast.refs_0_, bf16[1024,2048]{1,0:T(8,128)(2,1)} %get-tuple-element.43.refs_1_, bf16[1024,1024]{1,0:T(8,128)(2,1)} %get-tuple-element.44.refs_2_, bf16[256,2048]{1,0:T(8,128)(2,1)} %copy-done.2, ...), custom_call_target="tpu_custom_call" | custom-call | flops 4294967296 | bytes 4096 | tf_op jit(solution)/shard_map/pallas_call | solution.py:47
  159.0 9.1 %shard_map.134 = (bf16[1024,1024]{1,0:T(8,128)(2,1)}, bf16[1024,1024]{1,0:T(8,128)(2,1)}, f32[1,1024]{1,0:T(1,128)}) custom-call(s32[1]{0:T(128)} %bitcast.refs_0_, bf16[1024,2048]{1,0:T(8,128)(2,1)} %get-tuple-element.43.refs_1_, bf16[1024,1024]{1,0:T(8,128)(2,1)} %get-tuple-element.44.refs_2_, bf16[256,2048]{1,0:T(8,128)(2,1)} %copy-done.2, ...), custom_call_target="tpu_custom_call" | custom-call | flops 4294967296 | bytes 4096 | tf_op jit(solution)/shard_map/pallas_call | solution.py:47
  168.5 8.9 %shard_map.135 = (bf16[1024,1024]{1,0:T(8,128)(2,1)}, bf16[1024,1024]{1,0:T(8,128)(2,1)}) custom-call(s32[1]{0:T(128)} %bitcast.refs_0_, bf16[8,2,128,1024]{3,2,1,0:T(8,128)(2,1)} %bitcast.55, bf16[1024,1024]{1,0:T(8,128)(2,1)} %get-tuple-element.54.refs_2_.refs_0_, bf16[1024,1024]{1,0:T(8,128)(2,1)} %get-tuple-element.56.refs_3_.refs_1_, ...), custom_call_target="tpu_custom_call" | custom-call | flops 34359738368 | bytes 4096 | tf_op jit(solution)/shard_map/pallas_call | solution.py:47
  177.4 2.8 add_convert_fusion.1.refs_5_
  180.2 1.5 collective-permute-start.14
  181.7 1.6 add_convert_fusion.refs_6_
  183.4 3.4 %collective-permute-start.15 = (bf16[2,1,2,2,64,1024]{5,4,3,2,1,0:T(8,128)(2,1)}, bf16[2,1,2,2,64,1024]{5,4,3,2,1,0:T(8,128)(2,1)}, u32[]{:S(2)}, u32[]{:S(2)}) collective-permute-start(bf16[2,1,2,2,64,1024]{5,4,3,2,1,0:T(8,128)(2,1)} %add_convert_fusion.refs_6_), channel_id=1, source_target_pairs={{0,8},{2,10},{4,12},{6,14},{8,0},{10,2},{12,4},{14,6},{16,24},{18,... | collective-permute-start | bytes 3145736 | tf_op jit(solution)/shard_map/ppermute | solution.py:510
  186.8 15.8 %shard_map.136 = (bf16[1024,2048]{1,0:T(8,128)(2,1)}, bf16[512,2048]{1,0:T(8,128)(2,1)}, s32[1]{0:T(128)}) custom-call(bf16[1024,1024]{1,0:T(8,128)(2,1)} %get-tuple-element.54.refs_2_.refs_0_, bf16[1024,1024]{1,0:T(8,128)(2,1)} %get-tuple-element.56.refs_3_.refs_1_, bf16[2048,2048]{1,0:T(8,128)(2,1)} %refs_2_.3, f32[1024,1]{1,0:T(8,128)} %copy.16.refs_4_.refs_3_, ...), custom_call_target="tpu_custom_call" | custom-call | flops 10737418240 | bytes 4096 | tf_op jit(solution)/shard_map/pallas_call | solution.py:47
  202.6 3.1 fusion.13
  209.9 2.4 add_convert_fusion.7.refs_5_
  212.3 2.4 add_convert_fusion.6.refs_6_
  214.8 2.3 add_convert_fusion.5.refs_7_
  217.1 3.6 %collective-permute-done.15 = bf16[2,1,2,2,64,1024]{5,4,3,2,1,0:T(8,128)(2,1)} collective-permute-done((bf16[2,1,2,2,64,1024]{5,4,3,2,1,0:T(8,128)(2,1)}, bf16[2,1,2,2,64,1024]{5,4,3,2,1,0:T(8,128)(2,1)}, u32[]{:S(2)}, u32[]{:S(2)}) %collective-permute-start.15) | collective-permute-done | bytes 1048608 | tf_op jit(solution)/shard_map/ppermute | solution.py:510
  220.7 2.4 add_convert_fusion.4.refs_8_
  223.2 8.9 %shard_map.137 = (bf16[1024,2048]{1,0:T(8,128)(2,1)}, s32[1]{0:T(128)}) custom-call(s32[1]{0:T(128)} %bitcast.refs_0_, bf16[1024,2048]{1,0:T(8,128)(2,1)} %get-tuple-element.60.refs_1_, bf16[1024,1024]{1,0:T(8,128)(2,1)} %get-tuple-element.44.refs_2_, bf16[256,2048]{1,0:T(8,128)(2,1)} %collective-permute-done.10.refs_3_, ...), custom_call_target="tpu_custom_call" | custom-call | flops 4294967296 | bytes 4096 | tf_op jit(solution)/shard_map/pallas_call | solution.py:47
  232.7 8.9 %collective-permute-start.22 = (f32[8,2,2,64]{3,1,0,2:T(2,128)S(1)}, f32[8,2,2,64]{3,1,0,2:T(2,128)S(1)}, u32[]{:S(2)}, u32[]{:S(2)}) collective-permute-start(f32[8,2,2,64]{3,1,0,2:T(2,128)S(1)} %fusion.2), channel_id=1, source_target_pairs={{0,2},{2,0},{4,6},{6,4},{8,10},{10,8},{12,14},{14,12},{16,18},{18,... | collective-permute-start | bytes 24584 | tf_op jit(solution)/shard_map/ppermute | solution.py:551
  242.9 1.6 collective-permute-start.23
  244.5 11.5 %collective-permute-done.23 = f32[2,2,2,1,2,64]{5,4,3,2,1,0:T(2,128)S(1)} collective-permute-done((f32[2,2,2,1,2,64]{5,4,3,2,1,0:T(2,128)S(1)}, f32[2,2,2,1,2,64]{5,4,3,2,1,0:T(2,128)S(1)}, u32[]{:S(2)}, u32[]{:S(2)}) %collective-permute-start.23) | collective-permute-done | bytes 4128 | tf_op jit(solution)/shard_map/ppermute | solution.py:510
  260.2 2.1 collective-permute-start.25
  262.3 1.4 add_convert_fusion.8
  263.8 10.1 %collective-permute-done.25 = f32[2,1,1,1,2,64]{5,4,3,2,1,0:T(2,128)S(1)} collective-permute-done((f32[2,1,1,1,2,64]{5,4,3,2,1,0:T(2,128)S(1)}, f32[2,1,1,1,2,64]{5,4,3,2,1,0:T(2,128)S(1)}, u32[]{:S(2)}, u32[]{:S(2)}) %collective-permute-start.25) | collective-permute-done | bytes 1056 | tf_op jit(solution)/shard_map/ppermute | solution.py:510
  274.1 2.1 add_convert_fusion.9
  276.2 1.0 collective-permute-start.28
  277.2 1.2 collective-permute-done.26
  278.4 1.1 collective-permute-done.31
  279.5 1.3 add_convert_fusion.12
  281.3 4.4 %collective-permute-done.28 = bf16[2,1,1,1,64,1024]{5,4,3,2,1,0:T(8,128)(2,1)} collective-permute-done((bf16[2,1,1,1,64,1024]{5,4,3,2,1,0:T(8,128)(2,1)}, bf16[2,1,1,1,64,1024]{5,4,3,2,1,0:T(8,128)(2,1)}, u32[]{:S(2)}, u32[]{:S(2)}) %collective-permute-start.28) | collective-permute-done | bytes 262176 | tf_op jit(solution)/shard_map/ppermute | solution.py:510
  285.7 1.3 add_convert_fusion.13
  287.8 1.3 add_bitcast_fusion
  289.1 1.4 add_convert_fusion.10
  290.4 2.0 collective-permute-start.20
  292.9 1.3 add_bitcast_fusion.1
  294.2 1.3 add_convert_fusion.11
  295.5 1.5 collective-permute-start.17
  297.0 1.8 collective-permute-done.20
  298.9 1.2 add_convert_fusion.14
  300.1 3.1 collective-permute-start.21
  304.0 1.1 add_convert_fusion.15
  305.9 1.8 collective-permute-done.21
  307.7 1.2 add_bitcast_fusion.2
  308.9 2.3 collective-permute-done.18
  311.1 1.1 add_bitcast_fusion.3
  312.3 0.8 pad_maximum_fusion
  (86 shorter events, 7.9 us)
Async XLA Ops:
  0.7 3.4 %copy-start.12 = (s32[1,1024]{1,0:T(1,128)S(1)}, s32[1,1024]{1,0:T(1,128)}, u32[]{:S(2)}) copy-start(s32[1,1024]{1,0:T(1,128)} %refs_2_.2) | copy-start | bytes 12292
  2.5 27.5 %collective-permute-start = (bf16[256,2048]{1,0:T(8,128)(2,1)S(1)}, bf16[256,2048]{1,0:T(8,128)(2,1)S(1)}, u32[]{:S(2)}, u32[]{:S(2)}) collective-permute-start(bf16[256,2048]{1,0:T(8,128)(2,1)S(1)} %get-tuple-element.71), channel_id=1, source_target_pairs={{0,2},{2,0},{4,6},{6,4},{8,10},{10,8},{12,14},{14,12},{16,18},{18,... | collective-permute-start | bytes 3145736 | tf_op jit(solution)/shard_map/ppermute | solution.py:458
  2.5 27.4 %collective-permute-start.1 = (bf16[256,2048]{1,0:T(8,128)(2,1)S(1)}, bf16[256,2048]{1,0:T(8,128)(2,1)}, u32[]{:S(2)}, u32[]{:S(2)}) collective-permute-start(bf16[256,2048]{1,0:T(8,128)(2,1)S(1)} %get-tuple-element.70), channel_id=1, source_target_pairs={{0,30},{2,4},{4,2},{6,8},{8,6},{10,12},{12,10},{14,16},{16,14},{18... | collective-permute-start | bytes 3145736 | tf_op jit(solution)/shard_map/ppermute | solution.py:458
  29.9 1.0 copy-start.16
  55.2 9.7 %collective-permute-start.2 = (bf16[256,2048]{1,0:T(8,128)(2,1)S(1)}, bf16[256,2048]{1,0:T(8,128)(2,1)S(1)}, u32[]{:S(2)}, u32[]{:S(2)}) collective-permute-start(bf16[256,2048]{1,0:T(8,128)(2,1)S(1)} %get-tuple-element.69), channel_id=1, source_target_pairs={{0,2},{2,0},{4,6},{6,4},{8,10},{10,8},{12,14},{14,12},{16,18},{18,... | collective-permute-start | bytes 3145736 | tf_op jit(solution)/shard_map/ppermute | solution.py:458
  55.4 15.3 %collective-permute-start.3 = (bf16[256,2048]{1,0:T(8,128)(2,1)S(1)}, bf16[256,2048]{1,0:T(8,128)(2,1)}, u32[]{:S(2)}, u32[]{:S(2)}) collective-permute-start(bf16[256,2048]{1,0:T(8,128)(2,1)S(1)} %get-tuple-element.68), channel_id=1, source_target_pairs={{0,30},{2,4},{4,2},{6,8},{8,6},{10,12},{12,10},{14,16},{16,14},{18... | collective-permute-start | bytes 3145736 | tf_op jit(solution)/shard_map/ppermute | solution.py:458
  64.9 5.9 %copy-start.15 = (bf16[256,2048]{1,0:T(8,128)(2,1)}, bf16[256,2048]{1,0:T(8,128)(2,1)S(1)}, u32[]{:S(2)}) copy-start(bf16[256,2048]{1,0:T(8,128)(2,1)S(1)} %collective-permute-done.2.refs_2_) | copy-start | bytes 3145732
  111.1 37.5 %collective-permute-start.4 = (bf16[256,2048]{1,0:T(8,128)(2,1)}, bf16[256,2048]{1,0:T(8,128)(2,1)S(1)}, u32[]{:S(2)}, u32[]{:S(2)}) collective-permute-start(bf16[256,2048]{1,0:T(8,128)(2,1)} %get-tuple-element.75), channel_id=1, source_target_pairs={{0,2},{2,0},{4,6},{6,4},{8,10},{10,8},{12,14},{14,12},{16,18},{18,... | collective-permute-start | bytes 3145736 | tf_op jit(solution)/shard_map/ppermute | solution.py:458
  121.6 27.0 %collective-permute-start.5 = (bf16[256,2048]{1,0:T(8,128)(2,1)}, bf16[256,2048]{1,0:T(8,128)(2,1)S(1)}, u32[]{:S(2)}, u32[]{:S(2)}) collective-permute-start(bf16[256,2048]{1,0:T(8,128)(2,1)} %get-tuple-element.74), channel_id=1, source_target_pairs={{0,30},{2,4},{4,2},{6,8},{8,6},{10,12},{12,10},{14,16},{16,14},{18... | collective-permute-start | bytes 3145736 | tf_op jit(solution)/shard_map/ppermute | solution.py:458
  131.5 9.3 %collective-permute-start.6 = (bf16[1024,1024]{1,0:T(8,128)(2,1)}, bf16[1024,1024]{1,0:T(8,128)(2,1)S(1)}, u32[]{:S(2)}, u32[]{:S(2)}) collective-permute-start(bf16[1024,1024]{1,0:T(8,128)(2,1)} %get-tuple-element.50.refs_3_), channel_id=1, source_target_pairs={{0,2},{2,0},{4,6},{6,4},{8,10},{10,8},{12,14},{14,12},{16,18},{18,... | collective-permute-start | bytes 6291464 | tf_op jit(solution)/shard_map/ppermute | solution.py:534
  131.6 12.3 %collective-permute-start.7 = (bf16[1024,1024]{1,0:T(8,128)(2,1)}, bf16[1024,1024]{1,0:T(8,128)(2,1)S(1)}, u32[]{:S(2)}, u32[]{:S(2)}) collective-permute-start(bf16[1024,1024]{1,0:T(8,128)(2,1)} %get-tuple-element.51.refs_4_), channel_id=1, source_target_pairs={{0,2},{2,0},{4,6},{6,4},{8,10},{10,8},{12,14},{14,12},{16,18},{18,... | collective-permute-start | bytes 6291464 | tf_op jit(solution)/shard_map/ppermute | solution.py:534
  140.8 4.5 %copy-start.8 = (bf16[1024,1024]{1,0:T(8,128)(2,1)S(1)}, bf16[1024,1024]{1,0:T(8,128)(2,1)}, u32[]{:S(2)}) copy-start(bf16[1024,1024]{1,0:T(8,128)(2,1)} %get-tuple-element.53) | copy-start | bytes 6291460
  140.8 6.1 %copy-start.4 = (bf16[1024,1024]{1,0:T(8,128)(2,1)}, bf16[1024,1024]{1,0:T(8,128)(2,1)S(1)}, u32[]{:S(2)}) copy-start(bf16[1024,1024]{1,0:T(8,128)(2,1)S(1)} %collective-permute-done.6) | copy-start | bytes 6291460
  143.3 5.3 %copy-start.1 = (bf16[2,2,2,1,64,1024]{5,4,3,2,1,0:T(8,128)(2,1)}, bf16[2,2,2,1,64,1024]{5,4,3,2,1,0:T(8,128)(2,1)S(1)}, u32[]{:S(2)}) copy-start(bf16[2,2,2,1,64,1024]{5,4,3,2,1,0:T(8,128)(2,1)S(1)} %add_convert_fusion.3.refs_7_) | copy-start | bytes 3145732
  143.3 62.4 %collective-permute-start.12 = (bf16[2,2,2,1,64,1024]{5,4,3,2,1,0:T(8,128)(2,1)S(1)}, bf16[2,2,2,1,64,1024]{5,4,3,2,1,0:T(8,128)(2,1)}, u32[]{:S(2)}, u32[]{:S(2)}) collective-permute-start(bf16[2,2,2,1,64,1024]{5,4,3,2,1,0:T(8,128)(2,1)S(1)} %add_convert_fusion.3.refs_7_), channel_id=1, source_target_pairs={{0,1},{1,0},{2,3},{3,2},{4,5},{5,4},{6,7},{7,6},{8,9},{9,8},{10,11... | collective-permute-start | bytes 3145736 | tf_op jit(solution)/shard_map/ppermute | solution.py:510
  143.9 1.4 copy-start.7
  147.0 1.6 copy-start
  147.0 65.3 %collective-permute-start.13 = (bf16[2,2,1,2,64,1024]{5,4,3,2,1,0:T(8,128)(2,1)S(1)}, bf16[2,2,1,2,64,1024]{5,4,3,2,1,0:T(8,128)(2,1)}, u32[]{:S(2)}, u32[]{:S(2)}) collective-permute-start(bf16[2,2,1,2,64,1024]{5,4,3,2,1,0:T(8,128)(2,1)S(1)} %add_convert_fusion.2.refs_8_), channel_id=1, source_target_pairs={{0,4},{2,6},{4,0},{6,2},{8,12},{10,14},{12,8},{14,10},{16,20},{18,... | collective-permute-start | bytes 3145736 | tf_op jit(solution)/shard_map/ppermute | solution.py:510
  148.6 1.0 copy-start.2
  148.6 1.3 copy-start.3
  159.0 18.4 %collective-permute-start.8 = (bf16[1024,1024]{1,0:T(8,128)(2,1)}, bf16[1024,1024]{1,0:T(8,128)(2,1)S(1)}, u32[]{:S(2)}, u32[]{:S(2)}) collective-permute-start(bf16[1024,1024]{1,0:T(8,128)(2,1)} %get-tuple-element.55.refs_7_.refs_4_), channel_id=1, source_target_pairs={{0,2},{2,0},{4,6},{6,4},{8,10},{10,8},{12,14},{14,12},{16,18},{18,... | collective-permute-start | bytes 6291464 | tf_op jit(solution)/shard_map/ppermute | solution.py:534
  168.1 13.7 %collective-permute-start.9 = (bf16[1024,1024]{1,0:T(8,128)(2,1)}, bf16[1024,1024]{1,0:T(8,128)(2,1)S(1)}, u32[]{:S(2)}, u32[]{:S(2)}) collective-permute-start(bf16[1024,1024]{1,0:T(8,128)(2,1)} %get-tuple-element.57.refs_5_), channel_id=1, source_target_pairs={{0,2},{2,0},{4,6},{6,4},{8,10},{10,8},{12,14},{14,12},{16,18},{18,... | collective-permute-start | bytes 6291464 | tf_op jit(solution)/shard_map/ppermute | solution.py:534
  177.4 4.3 %copy-start.6 = (bf16[1024,1024]{1,0:T(8,128)(2,1)S(1)}, bf16[1024,1024]{1,0:T(8,128)(2,1)}, u32[]{:S(2)}) copy-start(bf16[1024,1024]{1,0:T(8,128)(2,1)} %get-tuple-element.59) | copy-start | bytes 6291460
  180.2 34.5 %collective-permute-start.14 = (bf16[2,2,2,1,64,1024]{5,4,3,2,1,0:T(8,128)(2,1)}, bf16[2,2,2,1,64,1024]{5,4,3,2,1,0:T(8,128)(2,1)}, u32[]{:S(2)}, u32[]{:S(2)}) collective-permute-start(bf16[2,2,2,1,64,1024]{5,4,3,2,1,0:T(8,128)(2,1)} %add_convert_fusion.1.refs_5_), channel_id=1, source_target_pairs={{0,1},{1,0},{2,3},{3,2},{4,5},{5,4},{6,7},{7,6},{8,9},{9,8},{10,11... | collective-permute-start | bytes 3145736 | tf_op jit(solution)/shard_map/ppermute | solution.py:510
  181.7 20.9 %copy-start.5 = (bf16[1024,1024]{1,0:T(8,128)(2,1)}, bf16[1024,1024]{1,0:T(8,128)(2,1)S(1)}, u32[]{:S(2)}) copy-start(bf16[1024,1024]{1,0:T(8,128)(2,1)S(1)} %collective-permute-done.9) | copy-start | bytes 6291460
  183.4 37.3 %collective-permute-start.15 = (bf16[2,1,2,2,64,1024]{5,4,3,2,1,0:T(8,128)(2,1)}, bf16[2,1,2,2,64,1024]{5,4,3,2,1,0:T(8,128)(2,1)}, u32[]{:S(2)}, u32[]{:S(2)}) collective-permute-start(bf16[2,1,2,2,64,1024]{5,4,3,2,1,0:T(8,128)(2,1)} %add_convert_fusion.refs_6_), channel_id=1, source_target_pairs={{0,8},{2,10},{4,12},{6,14},{8,0},{10,2},{12,4},{14,6},{16,24},{18,... | collective-permute-start | bytes 3145736 | tf_op jit(solution)/shard_map/ppermute | solution.py:510
  202.6 3.2 %copy-start.11 = (f32[1,2048]{1,0:T(1,128)S(1)}, f32[1,2048]{1,0:T(1,128)}, u32[]{:S(2)}) copy-start(f32[1,2048]{1,0:T(1,128)} %get-tuple-element.67) | copy-start | bytes 24580
  202.6 3.2 %copy-start.13 = (f32[1,1024]{1,0:T(1,128)S(1)}, f32[1,1024]{1,0:T(1,128)}, u32[]{:S(2)}) copy-start(f32[1,1024]{1,0:T(1,128)} %get-tuple-element.65) | copy-start | bytes 12292
  202.6 3.2 %copy-start.14 = (f32[1,1024]{1,0:T(1,128)S(1)}, f32[1,1024]{1,0:T(1,128)}, u32[]{:S(2)}) copy-start(f32[1,1024]{1,0:T(1,128)} %get-tuple-element.66) | copy-start | bytes 12292
  205.7 17.4 %collective-permute-start.10 = (bf16[256,2048]{1,0:T(8,128)(2,1)}, bf16[256,2048]{1,0:T(8,128)(2,1)}, u32[]{:S(2)}, u32[]{:S(2)}) collective-permute-start(bf16[256,2048]{1,0:T(8,128)(2,1)} %get-tuple-element.73), channel_id=1, source_target_pairs={{0,2},{2,0},{4,6},{6,4},{8,10},{10,8},{12,14},{14,12},{16,18},{18,... | collective-permute-start | bytes 3145736 | tf_op jit(solution)/shard_map/ppermute | solution.py:458
  205.7 17.4 %collective-permute-start.11 = (bf16[256,2048]{1,0:T(8,128)(2,1)}, bf16[256,2048]{1,0:T(8,128)(2,1)}, u32[]{:S(2)}, u32[]{:S(2)}) collective-permute-start(bf16[256,2048]{1,0:T(8,128)(2,1)} %get-tuple-element.72), channel_id=1, source_target_pairs={{0,30},{2,4},{4,2},{6,8},{8,6},{10,12},{12,10},{14,16},{16,14},{18... | collective-permute-start | bytes 3145736 | tf_op jit(solution)/shard_map/ppermute | solution.py:458
  223.2 33.2 %copy-start.10 = (bf16[2,1,2,1,64,1024]{5,4,3,2,1,0:T(8,128)(2,1)S(1)}, bf16[2,1,2,1,64,1024]{5,4,3,2,1,0:T(8,128)(2,1)}, u32[]{:S(2)}) copy-start(bf16[2,1,2,1,64,1024]{5,4,3,2,1,0:T(8,128)(2,1)} %add_convert_fusion.4.refs_8_) | copy-start | bytes 1572868
  223.2 35.6 %copy-start.9 = (bf16[2,1,2,1,64,1024]{5,4,3,2,1,0:T(8,128)(2,1)S(1)}, bf16[2,1,2,1,64,1024]{5,4,3,2,1,0:T(8,128)(2,1)}, u32[]{:S(2)}) copy-start(bf16[2,1,2,1,64,1024]{5,4,3,2,1,0:T(8,128)(2,1)} %add_convert_fusion.5.refs_7_) | copy-start | bytes 1572868
  232.7 10.1 %collective-permute-start.22 = (f32[8,2,2,64]{3,1,0,2:T(2,128)S(1)}, f32[8,2,2,64]{3,1,0,2:T(2,128)S(1)}, u32[]{:S(2)}, u32[]{:S(2)}) collective-permute-start(f32[8,2,2,64]{3,1,0,2:T(2,128)S(1)} %fusion.2), channel_id=1, source_target_pairs={{0,2},{2,0},{4,6},{6,4},{8,10},{10,8},{12,14},{14,12},{16,18},{18,... | collective-permute-start | bytes 24584 | tf_op jit(solution)/shard_map/ppermute | solution.py:551
  241.7 20.7 %collective-permute-start.30 = (bf16[2,2,1,1,64,1024]{5,4,3,2,1,0:T(8,128)(2,1)}, bf16[2,2,1,1,64,1024]{5,4,3,2,1,0:T(8,128)(2,1)}, u32[]{:S(2)}, u32[]{:S(2)}) collective-permute-start(bf16[2,2,1,1,64,1024]{5,4,3,2,1,0:T(8,128)(2,1)} %add_convert_fusion.6.refs_6_), channel_id=1, source_target_pairs={{0,1},{1,0},{2,3},{3,2},{4,5},{5,4},{6,7},{7,6},{8,9},{9,8},{10,11... | collective-permute-start | bytes 1572872 | tf_op jit(solution)/shard_map/ppermute | solution.py:510
  242.2 31.9 %collective-permute-start.27 = (bf16[2,2,1,1,64,1024]{5,4,3,2,1,0:T(8,128)(2,1)}, bf16[2,2,1,1,64,1024]{5,4,3,2,1,0:T(8,128)(2,1)}, u32[]{:S(2)}, u32[]{:S(2)}) collective-permute-start(bf16[2,2,1,1,64,1024]{5,4,3,2,1,0:T(8,128)(2,1)} %add_convert_fusion.7.refs_5_), channel_id=1, source_target_pairs={{0,4},{2,6},{4,0},{6,2},{8,12},{10,14},{12,8},{14,10},{16,20},{18,... | collective-permute-start | bytes 1572872 | tf_op jit(solution)/shard_map/ppermute | solution.py:510
  242.9 13.1 %collective-permute-start.23 = (f32[2,2,2,1,2,64]{5,4,3,2,1,0:T(2,128)S(1)}, f32[2,2,2,1,2,64]{5,4,3,2,1,0:T(2,128)S(1)}, u32[]{:S(2)}, u32[]{:S(2)}) collective-permute-start(f32[2,2,2,1,2,64]{5,4,3,2,1,0:T(2,128)S(1)} %constant_dynamic-slice_fusion.4), channel_id=1, source_target_pairs={{0,1},{1,0},{2,3},{3,2},{4,5},{5,4},{6,7},{7,6},{8,9},{9,8},{10,11... | collective-permute-start | bytes 12296 | tf_op jit(solution)/shard_map/ppermute | solution.py:510
  256.0 4.2 %collective-permute-start.24 = (f32[2,2,1,1,2,64]{5,4,3,2,1,0:T(2,128)S(1)}, f32[2,2,1,1,2,64]{5,4,3,2,1,0:T(2,128)S(1)}, u32[]{:S(2)}, u32[]{:S(2)}) collective-permute-start(f32[2,2,1,1,2,64]{5,4,3,2,1,0:T(2,128)S(1)} %fusion.3), channel_id=1, source_target_pairs={{0,4},{2,6},{4,0},{6,2},{8,12},{10,14},{12,8},{14,10},{16,20},{18,... | collective-permute-start | bytes 6152 | tf_op jit(solution)/shard_map/ppermute | solution.py:510
  256.3 32.7 %collective-permute-start.19 = (bf16[2,1,2,1,64,1024]{5,4,3,2,1,0:T(8,128)(2,1)S(1)}, bf16[2,1,2,1,64,1024]{5,4,3,2,1,0:T(8,128)(2,1)}, u32[]{:S(2)}, u32[]{:S(2)}) collective-permute-start(bf16[2,1,2,1,64,1024]{5,4,3,2,1,0:T(8,128)(2,1)S(1)} %copy-done.10), channel_id=1, source_target_pairs={{0,1},{1,0},{2,3},{3,2},{4,5},{5,4},{6,7},{7,6},{8,9},{9,8},{10,11... | collective-permute-start | bytes 1572872 | tf_op jit(solution)/shard_map/ppermute | solution.py:510
  258.8 35.4 %collective-permute-start.16 = (bf16[2,1,2,1,64,1024]{5,4,3,2,1,0:T(8,128)(2,1)S(1)}, bf16[2,1,2,1,64,1024]{5,4,3,2,1,0:T(8,128)(2,1)}, u32[]{:S(2)}, u32[]{:S(2)}) collective-permute-start(bf16[2,1,2,1,64,1024]{5,4,3,2,1,0:T(8,128)(2,1)S(1)} %copy-done.9), channel_id=1, source_target_pairs={{0,8},{2,10},{4,12},{6,14},{8,0},{10,2},{12,4},{14,6},{16,24},{18,... | collective-permute-start | bytes 1572872 | tf_op jit(solution)/shard_map/ppermute | solution.py:510
  260.2 13.6 %collective-permute-start.25 = (f32[2,1,1,1,2,64]{5,4,3,2,1,0:T(2,128)S(1)}, f32[2,1,1,1,2,64]{5,4,3,2,1,0:T(2,128)S(1)}, u32[]{:S(2)}, u32[]{:S(2)}) collective-permute-start(f32[2,1,1,1,2,64]{5,4,3,2,1,0:T(2,128)S(1)} %fusion.5), channel_id=1, source_target_pairs={{0,8},{2,10},{4,12},{6,14},{8,0},{10,2},{12,4},{14,6},{16,24},{18,... | collective-permute-start | bytes 3080 | tf_op jit(solution)/shard_map/ppermute | solution.py:510
  263.7 15.8 %collective-permute-start.31 = (bf16[2,1,1,1,64,1024]{5,4,3,2,1,0:T(8,128)(2,1)S(1)}, bf16[2,1,1,1,64,1024]{5,4,3,2,1,0:T(8,128)(2,1)}, u32[]{:S(2)}, u32[]{:S(2)}) collective-permute-start(bf16[2,1,1,1,64,1024]{5,4,3,2,1,0:T(8,128)(2,1)S(1)} %add_convert_fusion.8), channel_id=1, source_target_pairs={{0,8},{2,10},{4,12},{6,14},{8,0},{10,2},{12,4},{14,6},{16,24},{18,... | collective-permute-start | bytes 786440 | tf_op jit(solution)/shard_map/ppermute | solution.py:510
  273.8 4.5 %collective-permute-start.26 = (f32[1,1,1,1,2,64]{5,4,3,2,1,0:T(2,128)S(1)}, f32[1,1,1,1,2,64]{5,4,3,2,1,0:T(2,128)S(1)}, u32[]{:S(2)}, u32[]{:S(2)}) collective-permute-start(f32[1,1,1,1,2,64]{5,4,3,2,1,0:T(2,128)S(1)} %fusion.10), channel_id=1, source_target_pairs={{0,16},{2,18},{4,20},{6,22},{8,24},{10,26},{12,28},{14,30},{16,0},... | collective-permute-start | bytes 1544 | tf_op jit(solution)/shard_map/ppermute | solution.py:510
  276.2 9.6 %collective-permute-start.28 = (bf16[2,1,1,1,64,1024]{5,4,3,2,1,0:T(8,128)(2,1)}, bf16[2,1,1,1,64,1024]{5,4,3,2,1,0:T(8,128)(2,1)}, u32[]{:S(2)}, u32[]{:S(2)}) collective-permute-start(bf16[2,1,1,1,64,1024]{5,4,3,2,1,0:T(8,128)(2,1)} %add_convert_fusion.9), channel_id=1, source_target_pairs={{0,8},{2,10},{4,12},{6,14},{8,0},{10,2},{12,4},{14,6},{16,24},{18,... | collective-permute-start | bytes 786440 | tf_op jit(solution)/shard_map/ppermute | solution.py:510
  280.7 7.0 %collective-permute-start.32 = (bf16[1,1,1,1,64,1024]{5,4,3,2,1,0:T(8,128)(2,1)S(1)}, bf16[1,1,1,1,64,1024]{5,4,3,2,1,0:T(8,128)(2,1)S(1)}, u32[]{:S(2)}, u32[]{:S(2)}) collective-permute-start(bf16[1,1,1,1,64,1024]{5,4,3,2,1,0:T(8,128)(2,1)S(1)} %add_convert_fusion.12), channel_id=1, source_target_pairs={{0,16},{2,18},{4,20},{6,22},{8,24},{10,26},{12,28},{14,30},{16,0},... | collective-permute-start | bytes 393224 | tf_op jit(solution)/shard_map/ppermute | solution.py:510
  287.0 5.9 %collective-permute-start.29 = (bf16[1,1,1,1,64,1024]{5,4,3,2,1,0:T(8,128)(2,1)S(1)}, bf16[1,1,1,1,64,1024]{5,4,3,2,1,0:T(8,128)(2,1)S(1)}, u32[]{:S(2)}, u32[]{:S(2)}) collective-permute-start(bf16[1,1,1,1,64,1024]{5,4,3,2,1,0:T(8,128)(2,1)S(1)} %add_convert_fusion.13), channel_id=1, source_target_pairs={{0,16},{2,18},{4,20},{6,22},{8,24},{10,26},{12,28},{14,30},{16,0},... | collective-permute-start | bytes 393224 | tf_op jit(solution)/shard_map/ppermute | solution.py:510
  290.4 8.4 %collective-permute-start.20 = (bf16[2,1,1,1,64,1024]{5,4,3,2,1,0:T(8,128)(2,1)S(1)}, bf16[2,1,1,1,64,1024]{5,4,3,2,1,0:T(8,128)(2,1)S(1)}, u32[]{:S(2)}, u32[]{:S(2)}) collective-permute-start(bf16[2,1,1,1,64,1024]{5,4,3,2,1,0:T(8,128)(2,1)S(1)} %add_convert_fusion.10), channel_id=1, source_target_pairs={{0,4},{2,6},{4,0},{6,2},{8,12},{10,14},{12,8},{14,10},{16,20},{18,... | collective-permute-start | bytes 786440 | tf_op jit(solution)/shard_map/ppermute | solution.py:510
  295.5 8.4 %collective-permute-start.17 = (bf16[2,1,1,1,64,1024]{5,4,3,2,1,0:T(8,128)(2,1)S(1)}, bf16[2,1,1,1,64,1024]{5,4,3,2,1,0:T(8,128)(2,1)S(1)}, u32[]{:S(2)}, u32[]{:S(2)}) collective-permute-start(bf16[2,1,1,1,64,1024]{5,4,3,2,1,0:T(8,128)(2,1)S(1)} %add_convert_fusion.11), channel_id=1, source_target_pairs={{0,4},{2,6},{4,0},{6,2},{8,12},{10,14},{12,8},{14,10},{16,20},{18,... | collective-permute-start | bytes 786440 | tf_op jit(solution)/shard_map/ppermute | solution.py:510
  300.1 7.6 %collective-permute-start.21 = (bf16[1,1,1,1,64,1024]{5,4,3,2,1,0:T(8,128)(2,1)S(1)}, bf16[1,1,1,1,64,1024]{5,4,3,2,1,0:T(8,128)(2,1)S(1)}, u32[]{:S(2)}, u32[]{:S(2)}) collective-permute-start(bf16[1,1,1,1,64,1024]{5,4,3,2,1,0:T(8,128)(2,1)S(1)} %add_convert_fusion.14), channel_id=1, source_target_pairs={{0,16},{2,18},{4,20},{6,22},{8,24},{10,26},{12,28},{14,30},{16,0},... | collective-permute-start | bytes 393224 | tf_op jit(solution)/shard_map/ppermute | solution.py:510
  305.1 6.0 %collective-permute-start.18 = (bf16[1,1,1,1,64,1024]{5,4,3,2,1,0:T(8,128)(2,1)S(1)}, bf16[1,1,1,1,64,1024]{5,4,3,2,1,0:T(8,128)(2,1)S(1)}, u32[]{:S(2)}, u32[]{:S(2)}) collective-permute-start(bf16[1,1,1,1,64,1024]{5,4,3,2,1,0:T(8,128)(2,1)S(1)} %add_convert_fusion.15), channel_id=1, source_target_pairs={{0,16},{2,18},{4,20},{6,22},{8,24},{10,26},{12,28},{14,30},{16,0},... | collective-permute-start | bytes 393224 | tf_op jit(solution)/shard_map/ppermute | solution.py:510
